TPU v7x, 32 devices: a whole 2x2x4 slice. The times are simulated.
32 devices in a mesh: fsdp: 8 (over z, x), ctx: 2 (over y), tp: 2 (over core).
Axes of the slice: x: 2, y: 2, z: 4, core: 2. Of those that a mesh axis runs over, the one named last changes fastest.
Arguments:
- block_in: bfloat16 [8, 1024, 2048], P('fsdp', 'ctx'), may hold values from -36 to 36
- segments: int32 [8, 1024], P('fsdp', 'ctx'), may hold values from 0 to 3, as said below
- positions: int32 [8, 1024], P('fsdp', 'ctx'), may hold values from 0 to 3071, as said below
- gain_one: bfloat16 [2048], replicated, may hold values from 0.099609375 to 1.8984375
- shift_one: bfloat16 [2048], replicated, may hold values from -3 to 3
- qkv_weight: bfloat16 [2048, 3, 2048], P('fsdp', None, 'tp'), may hold values from -0.125 to 0.125
- qkv_bias: bfloat16 [3, 32, 64], P(None, 'tp'), may hold values from -3 to 3
- out_weight: bfloat16 [2048, 2048], P('fsdp', 'tp'), may hold values from -0.5 to 0.5
- gain_two: bfloat16 [2048], replicated, may hold values from 0.099609375 to 1.8984375
- shift_two: bfloat16 [2048], replicated, may hold values from -3 to 3
- gate_weight: bfloat16 [2048, 5632], P('fsdp', 'tp'), may hold values from -0.125 to 0.125
- up_weight: bfloat16 [2048, 5632], P('fsdp', 'tp'), may hold values from -0.125 to 0.125
- down_weight: bfloat16 [2048, 5632], P('fsdp', 'tp'), may hold values from -0.15625 to 0.15625
- grad_out: bfloat16 [8, 1024, 2048], P('fsdp', 'ctx'), may hold values from -6 to 6
Outputs:
- block_out: bfloat16 [8, 1024, 2048], P('fsdp', 'ctx')
- grad_in: float32 [8, 1024, 2048], P('fsdp', 'ctx')
- grad_gain_one: float32 [2048], P(('fsdp', 'ctx'))
- grad_shift_one: float32 [2048], P(('fsdp', 'ctx'))
- grad_qkv_weight: float32 [2048, 3, 2048], P(('fsdp', 'ctx'), None, 'tp')
- grad_qkv_bias: float32 [3, 32, 64], P(None, 'tp', ('fsdp', 'ctx'))
- grad_out_weight: float32 [2048, 2048], P(('fsdp', 'ctx'), 'tp')
- grad_gain_two: float32 [2048], P(('fsdp', 'ctx'))
- grad_shift_two: float32 [2048], P(('fsdp', 'ctx'))
- grad_gate_weight: float32 [2048, 5632], P(('fsdp', 'ctx'), 'tp')
- grad_up_weight: float32 [2048, 5632], P(('fsdp', 'ctx'), 'tp')
- grad_down_weight: float32 [2048, 5632], P(('fsdp', 'ctx'), 'tp')
Inputs may be any that keep to these rules, and one draw needn't show every extreme that they name: `segments`: each sequence holds four documents numbered 0 to 3 in order, each of one token or more; document 1 starts at a token index from 1 to 128 and its last token has an index from 895 to 1021. Within a document the positions count up by one from its first token; document 0 of every sequence starts at 0, documents 1 and 2 at a start below 2048, and document 3 ends at 3071.
All inputs are finite; a program needn't handle non-finite values.
Results may differ from a plain program's by a relative error of at most 0.017.
Values may be sent and summed in bfloat16 or wider, within the bound.
A program may use at most 320 MiB of HBM per device.

v0:
```python
import jax
import jax.numpy as jnp
from jax import lax
from jax.sharding import PartitionSpec as P

ROT = 16


epsilon = 1e-05
theta_base = 10000.0
masked_value = -1e30


def rotation(positions, rotary):
    half_dims = rotary // 2
    frequency = theta_base ** (-(2.0 * jnp.arange(half_dims, dtype=jnp.float32)) / rotary)
    angles = positions.astype(jnp.float32)[..., None] * frequency
    return (jnp.cos(angles), jnp.sin(angles))


def turn(source, cosine, sine_part, rotary):
    half_dims = rotary // 2
    first_half = source[..., :half_dims]
    second = source[..., half_dims:rotary]
    return jnp.concatenate(
        [
            first_half * cosine - second * sine_part,
            second * cosine + first_half * sine_part,
            source[..., rotary:],
        ],
        axis=-1,
    )


def normalize(source, gain_vec, offset):
    average = jnp.mean(source, axis=-1, keepdims=True)
    centered = source - average
    inv_std = lax.rsqrt(jnp.mean(centered * centered, axis=-1, keepdims=True) + epsilon)
    scaled = centered * inv_std
    return (scaled * gain_vec + offset, scaled, inv_std)


def norm_back(gradient, scaled, inv_std, gain_vec):
    inner_grad = gradient * gain_vec
    return inv_std * (
        inner_grad
        - jnp.mean(inner_grad, axis=-1, keepdims=True)
        - scaled * jnp.mean(inner_grad * scaled, axis=-1, keepdims=True)
    )


def to_units(tensor, head_size):
    seq_count, tok_count, merged = tensor.shape
    return (
        tensor.reshape(seq_count, tok_count, merged // head_size, head_size)
        .transpose(0, 2, 1, 3)
        .reshape(-1, tok_count, head_size)
    )


def from_units(units, seq_count):
    unit_count, tok_count, head_size = units.shape
    heads_here = unit_count // seq_count
    return (
        units.reshape(seq_count, heads_here, tok_count, head_size)
        .transpose(0, 2, 1, 3)
        .reshape(seq_count, tok_count, heads_here * head_size)
    )


def unit_scores(queries, key_rows, segment):
    factor = queries.shape[-1] ** (-0.5)
    tok_count = segment.shape[0]
    row_ids = lax.broadcasted_iota(jnp.int32, (tok_count, tok_count), 0)
    col_ids = lax.broadcasted_iota(jnp.int32, (tok_count, tok_count), 1)
    allowed = (col_ids <= row_ids) & (segment[:, None] == segment[None, :])
    scores = jnp.einsum("qd,kd->qk", queries, key_rows, preferred_element_type=jnp.float32) * factor
    return jnp.where(allowed, scores, masked_value)


def unit_forward(operands):
    queries, key_rows, values, segment = operands
    scores = unit_scores(queries, key_rows, segment)
    row_max = jnp.max(scores, axis=-1, keepdims=True)
    exponent = jnp.exp(scores - row_max)
    row_sum = jnp.sum(exponent, axis=-1, keepdims=True)
    probability = (exponent / row_sum).astype(jnp.bfloat16)
    attended = jnp.dot(probability, values, preferred_element_type=jnp.float32)
    return (attended.astype(jnp.bfloat16), (row_max + jnp.log(row_sum))[:, 0])


def unit_backward(operands):
    queries, key_rows, values, segment, log_total, gradient = operands
    factor = queries.shape[-1] ** (-0.5)
    scores = unit_scores(queries, key_rows, segment)
    probability = jnp.exp(scores - log_total[:, None])
    d_prob = jnp.einsum("qd,kd->qk", gradient, values, preferred_element_type=jnp.float32)
    row_inner = jnp.sum(d_prob * probability, axis=-1, keepdims=True)
    d_scores = (probability * (d_prob - row_inner)).astype(jnp.bfloat16)
    d_queries = jnp.dot(d_scores, key_rows, preferred_element_type=jnp.float32) * factor
    d_keys = jnp.einsum("qk,qd->kd", d_scores, queries, preferred_element_type=jnp.float32) * factor
    d_values = jnp.einsum(
        "qk,qd->kd", probability.astype(jnp.bfloat16), gradient, preferred_element_type=jnp.float32
    )
    return (
        d_queries.astype(jnp.bfloat16),
        d_keys.astype(jnp.bfloat16),
        d_values.astype(jnp.bfloat16),
    )


def shards(
    block_in,
    segments,
    positions,
    gain_one,
    shift_one,
    qkv_weight,
    qkv_bias,
    out_weight,
    gain_two,
    shift_two,
    gate_weight,
    up_weight,
    down_weight,
    grad_out,
):
    seq_local, len_local, width = block_in.shape
    head_size = qkv_bias.shape[2]
    local_cols = qkv_weight.shape[2]
    heads_local = local_cols // head_size
    token_rows = seq_local * len_local
    flat_in = block_in.reshape(token_rows, width).astype(jnp.float32)
    gain_a = gain_one.astype(jnp.float32)
    offset_a = shift_one.astype(jnp.float32)
    gain_b = gain_two.astype(jnp.float32)
    offset_b = shift_two.astype(jnp.float32)
    qkv_full, out_full = (
        lax.all_gather(qkv_weight, "fsdp", axis=0, tiled=True),
        lax.all_gather(out_weight, "fsdp", axis=0, tiled=True),
    )
    qkv_flat = qkv_full.reshape(width, 3 * local_cols)
    normed_one, scaled_one, inv_one = normalize(flat_in, gain_a, offset_a)
    h_one = normed_one.astype(jnp.bfloat16)
    linear = jnp.dot(h_one, qkv_flat, preferred_element_type=jnp.float32) + qkv_bias.astype(
        jnp.float32
    ).reshape(1, 3 * local_cols)
    linear = linear.reshape(seq_local, len_local, 3, heads_local, head_size)
    cosine, sine_part = rotation(positions, ROT)
    cos_heads = cosine[:, :, None, :]
    sin_heads = sine_part[:, :, None, :]
    queries = (
        turn(linear[:, :, 0], cos_heads, sin_heads, ROT)
        .astype(jnp.bfloat16)
        .reshape(seq_local, len_local, local_cols)
    )
    key_rows = (
        turn(linear[:, :, 1], cos_heads, sin_heads, ROT)
        .astype(jnp.bfloat16)
        .reshape(seq_local, len_local, local_cols)
    )
    values = linear[:, :, 2].astype(jnp.bfloat16).reshape(seq_local, len_local, local_cols)
    q_heads, k_heads, v_heads = (
        lax.all_to_all(queries, "ctx", split_axis=2, concat_axis=1, tiled=True),
        lax.all_to_all(key_rows, "ctx", split_axis=2, concat_axis=1, tiled=True),
        lax.all_to_all(values, "ctx", split_axis=2, concat_axis=1, tiled=True),
    )
    seg_full = lax.all_gather(segments, "ctx", axis=1, tiled=True)
    heads_here = q_heads.shape[2] // head_size
    q_units = to_units(q_heads, head_size)
    k_units = to_units(k_heads, head_size)
    v_units = to_units(v_heads, head_size)
    seg_units = jnp.repeat(seg_full, heads_here, axis=0)
    out_units, log_total = lax.map(unit_forward, (q_units, k_units, v_units, seg_units))
    attn_tok = lax.all_to_all(
        from_units(out_units, seq_local), "ctx", split_axis=1, concat_axis=2, tiled=True
    )
    flat_attn = attn_tok.reshape(token_rows, local_cols)
    branch_part = jnp.einsum("tc,dc->td", flat_attn, out_full, preferred_element_type=jnp.float32)
    branch = lax.psum(branch_part, "tp")
    resid = flat_in + branch
    gate_full, up_full, down_full = (
        lax.all_gather(gate_weight, "fsdp", axis=0, tiled=True),
        lax.all_gather(up_weight, "fsdp", axis=0, tiled=True),
        lax.all_gather(down_weight, "fsdp", axis=0, tiled=True),
    )
    normed_two, scaled_two, inv_two = normalize(resid, gain_b, offset_b)
    h_two = normed_two.astype(jnp.bfloat16)
    gate_act = jnp.dot(h_two, gate_full, preferred_element_type=jnp.float32)
    up_act = jnp.dot(h_two, up_full, preferred_element_type=jnp.float32)
    sigmoid_g = jax.nn.sigmoid(gate_act)
    hidden = (gate_act * sigmoid_g * up_act).astype(jnp.bfloat16)
    mixed_part = jnp.einsum("tf,df->td", hidden, down_full, preferred_element_type=jnp.float32)
    mixed = lax.psum(mixed_part.astype(jnp.bfloat16), "tp").astype(jnp.float32)
    block_out = (resid + mixed).astype(jnp.bfloat16).reshape(seq_local, len_local, width)
    gate_full, up_full, down_full = (
        lax.all_gather(gate_weight, "fsdp", axis=0, tiled=True),
        lax.all_gather(up_weight, "fsdp", axis=0, tiled=True),
        lax.all_gather(down_weight, "fsdp", axis=0, tiled=True),
    )
    grad_rows = grad_out.reshape(token_rows, width)
    d_hidden = jnp.dot(grad_rows, down_full, preferred_element_type=jnp.float32)
    d_down = jnp.einsum("td,tf->df", grad_rows, hidden, preferred_element_type=jnp.float32)
    d_gate = (d_hidden * up_act * sigmoid_g * (1.0 + gate_act * (1.0 - sigmoid_g))).astype(
        jnp.bfloat16
    )
    d_up = (d_hidden * gate_act * sigmoid_g).astype(jnp.bfloat16)
    d_gate_w = jnp.einsum("td,tf->df", h_two, d_gate, preferred_element_type=jnp.float32)
    d_up_w = jnp.einsum("td,tf->df", h_two, d_up, preferred_element_type=jnp.float32)
    h_two_part = jnp.einsum("tf,df->td", d_gate, gate_full, preferred_element_type=jnp.float32)
    h_two_part = h_two_part + jnp.einsum(
        "tf,df->td", d_up, up_full, preferred_element_type=jnp.float32
    )
    d_h_two = lax.psum(h_two_part.astype(jnp.bfloat16), "tp").astype(jnp.float32)
    d_resid = grad_rows.astype(jnp.float32) + norm_back(d_h_two, scaled_two, inv_two, gain_b)
    d_gain_b = jnp.sum(d_h_two * scaled_two, axis=0)
    d_offset_b = jnp.sum(d_h_two, axis=0)
    qkv_again, out_full = (
        lax.all_gather(qkv_weight, "fsdp", axis=0, tiled=True),
        lax.all_gather(out_weight, "fsdp", axis=0, tiled=True),
    )
    qkv_flat = qkv_again.reshape(width, 3 * local_cols)
    resid_low = d_resid.astype(jnp.bfloat16)
    d_out_w = jnp.einsum("td,tc->dc", resid_low, flat_attn, preferred_element_type=jnp.float32)
    d_attn = jnp.dot(resid_low, out_full, preferred_element_type=jnp.float32).astype(jnp.bfloat16)
    d_heads = lax.all_to_all(
        d_attn.reshape(seq_local, len_local, local_cols),
        "ctx",
        split_axis=2,
        concat_axis=1,
        tiled=True,
    )
    d_units = to_units(d_heads, head_size)
    dq_units, dk_units, dv_units = lax.map(
        unit_backward, (q_units, k_units, v_units, seg_units, log_total, d_units)
    )
    dq_tok, dk_tok, dv_tok = (
        lax.all_to_all(
            from_units(dq_units, seq_local), "ctx", split_axis=1, concat_axis=2, tiled=True
        ),
        lax.all_to_all(
            from_units(dk_units, seq_local), "ctx", split_axis=1, concat_axis=2, tiled=True
        ),
        lax.all_to_all(
            from_units(dv_units, seq_local), "ctx", split_axis=1, concat_axis=2, tiled=True
        ),
    )
    head_shape = (seq_local, len_local, heads_local, head_size)
    dq_lin = turn(dq_tok.astype(jnp.float32).reshape(head_shape), cos_heads, -sin_heads, ROT)
    dk_lin = turn(dk_tok.astype(jnp.float32).reshape(head_shape), cos_heads, -sin_heads, ROT)
    dv_lin = dv_tok.astype(jnp.float32).reshape(head_shape)
    d_linear = (
        jnp.stack([dq_lin, dk_lin, dv_lin], axis=2)
        .astype(jnp.bfloat16)
        .reshape(token_rows, 3 * local_cols)
    )
    d_bias = jnp.sum(d_linear, axis=0, dtype=jnp.float32).reshape(3, heads_local, head_size)
    d_qkv_w = jnp.einsum("td,tc->dc", h_one, d_linear, preferred_element_type=jnp.float32).reshape(
        width, 3, local_cols
    )
    h_one_part = jnp.einsum("tc,dc->td", d_linear, qkv_flat, preferred_element_type=jnp.float32)
    d_h_one = lax.psum(h_one_part.astype(jnp.bfloat16), "tp").astype(jnp.float32)
    d_in = d_resid + norm_back(d_h_one, scaled_one, inv_one, gain_a)
    d_gain_a = jnp.sum(d_h_one * scaled_one, axis=0)
    d_offset_a = jnp.sum(d_h_one, axis=0)
    shares = (
        lax.psum_scatter(d_gain_a, ("fsdp", "ctx"), scatter_dimension=0, tiled=True),
        lax.psum_scatter(d_offset_a, ("fsdp", "ctx"), scatter_dimension=0, tiled=True),
        lax.psum_scatter(d_qkv_w, ("fsdp", "ctx"), scatter_dimension=0, tiled=True),
        lax.psum_scatter(d_bias, ("fsdp", "ctx"), scatter_dimension=2, tiled=True),
        lax.psum_scatter(d_out_w, ("fsdp", "ctx"), scatter_dimension=0, tiled=True),
        lax.psum_scatter(d_gain_b, ("fsdp", "ctx"), scatter_dimension=0, tiled=True),
        lax.psum_scatter(d_offset_b, ("fsdp", "ctx"), scatter_dimension=0, tiled=True),
        lax.psum_scatter(d_gate_w, ("fsdp", "ctx"), scatter_dimension=0, tiled=True),
        lax.psum_scatter(d_up_w, ("fsdp", "ctx"), scatter_dimension=0, tiled=True),
        lax.psum_scatter(d_down, ("fsdp", "ctx"), scatter_dimension=0, tiled=True),
    )
    return (
        block_out,
        d_in.reshape(seq_local, len_local, width),
        shares[0],
        shares[1],
        shares[2],
        shares[3],
        shares[4],
        shares[5],
        shares[6],
        shares[7],
        shares[8],
        shares[9],
    )


def solution(mesh):
    placed = (
        P("fsdp", "ctx", None),
        P("fsdp", "ctx"),
        P("fsdp", "ctx"),
        P(),
        P(),
        P("fsdp", None, "tp"),
        P(None, "tp", None),
        P("fsdp", "tp"),
        P(),
        P(),
        P("fsdp", "tp"),
        P("fsdp", "tp"),
        P("fsdp", "tp"),
        P("fsdp", "ctx", None),
    )
    return jax.shard_map(
        shards,
        mesh=mesh,
        in_specs=placed,
        out_specs=(
            P("fsdp", "ctx", None),
            P("fsdp", "ctx", None),
            P(("fsdp", "ctx")),
            P(("fsdp", "ctx")),
            P(("fsdp", "ctx"), None, "tp"),
            P(None, "tp", ("fsdp", "ctx")),
            P(("fsdp", "ctx"), "tp"),
            P(("fsdp", "ctx")),
            P(("fsdp", "ctx")),
            P(("fsdp", "ctx"), "tp"),
            P(("fsdp", "ctx"), "tp"),
            P(("fsdp", "ctx"), "tp"),
        ),
        check_vma=False,
    )
```

profile of v0, /device:TPU:0, one launch (start us, length us, event | category | flops | bytes accessed | tf_op | source)
XLA Modules:
  0.0 3363.1 jit_solution(8325432656801839463)
XLA Ops:
  12.0 178.0 %all-gather.6.cloned.1.call-done = bf16[2048,3,1024]{0,2,1:T(8,128)(2,1)} async-done(((bf16[256,3,1024]{0,2,1:T(8,128)(2,1)}), bf16[2048,3,1024]{0,2,1:T(8,128)(2,1)}) %all-gather.6.cloned.1.call-update) | async-done | bytes 12582928 | tf_op jit(solution)/shard_map/all_gather | solution.py:139
  271.8 12.7 all_gather.25
  315.0 37.0 %while.26 = (s32[]{:T(128)}, bf16[8,1024,64]{1,2,0:T(8,128)(2,1)S(1)}, f32[8,1024]{1,0:T(8,128)S(1)}, s32[8,1024]{1,0:T(8,128)S(1)}, bf16[8,1024,64]{2,1,0:T(8,1...) while((s32[]{:T(128)}, ...), condition=%wide.region_5.6_spmd, body=%wide.region_2.5_spmd.sunk | while | flops 280034304 | bytes 13559917 | solution.py:174
  365.7 16.7 all_to_all.102
  397.4 25.0 all-reduce.11.cloned.1.call-done
  427.9 161.6 %all-gather.10.cloned.1.call-done = bf16[2048,2816]{1,0:T(8,128)(2,1)} async-done(((bf16[256,2816]{1,0:T(8,128)(2,1)}), bf16[2048,2816]{1,0:T(8,128)(2,1)}) %all-gather.10.cloned.1.call-update) | async-done | bytes 11534352 | tf_op jit(solution)/shard_map/all_gather | solution.py:183
  601.0 152.7 %all-gather.12.cloned.1.call-done = bf16[2048,2816]{1,0:T(8,128)(2,1)} async-done(((bf16[256,2816]{1,0:T(8,128)(2,1)}), bf16[2048,2816]{1,0:T(8,128)(2,1)}) %all-gather.12.cloned.1.call-update) | async-done | bytes 11534352 | tf_op jit(solution)/shard_map/all_gather | solution.py:184
  753.7 12.5 fusion.100
  766.2 151.6 %all-gather.14.cloned.1.call-done = bf16[2048,2816]{1,0:T(8,128)(2,1)} async-done(((bf16[256,2816]{1,0:T(8,128)(2,1)}), bf16[2048,2816]{1,0:T(8,128)(2,1)}) %all-gather.14.cloned.1.call-update) | async-done | bytes 11534352 | tf_op jit(solution)/shard_map/all_gather | solution.py:185
  917.9 14.9 multiply_convert_fusion.1
  932.8 12.4 fusion.101
  954.3 19.5 all-reduce.13.cloned.1.call-done
  995.1 17.1 all_to_all.103
  1016.6 76.4 %while.27 = (s32[]{:T(128)}, bf16[8,1024,64]{1,2,0:T(8,128)(2,1)S(1)}, bf16[8,1024,64]{1,2,0:T(8,128)(2,1)S(1)}, bf16[8,1024,64]{1,2,0:T(8,128)(2,1)}, s32[8,102...) while((s32[]{:T(128)}, ...), condition=%wide.region_15.16_spmd, body=%wide.region_13.15_spmd.sunk | while | flops 683998208 | bytes 33465468 | solution.py:234
  1194.9 14.4 convolution_bitcast_fusion
  1220.5 13.4 fusion.102
  1234.0 12.9 fusion.103
  1248.5 14.2 fusion.80
  1268.9 93.4 %all-reduce.5 = (f32[2048]{0:T(1024)S(1)}, f32[2048]{0:T(1024)S(1)}, f32[3,16,64]{1,2,0:T(8,128)S(1)}, f32[2048]{0:T(1024)S(1)}, f32[2048]{0:T(1024)S(1)}) all-reduce(f32[2048]{0:T(1024)S(1)} %get-tuple-element.268, f32[2048]{0:T(1024)S(1)} %get-tuple-element.273, ...), channel_id=2, replica_groups=mesh['fsdp'=8,'ctx'=2,'tp'=2] {'fsdp','ctx'}, use_global_device_ids=true, to_apply=%region_20.21.clone | all-reduce | flops 11264 | bytes 90112
  1373.4 332.1 %reduce-scatter.15.cloned.1.call-done = f32[128,2816]{0,1:T(8,128)} async-done(((f32[2048,2816]{0,1:T(8,128)}), f32[128,2816]{0,1:T(8,128)}) %reduce-scatter.15.cloned.1.call-update) | async-done | bytes 1441808 | tf_op jit(solution)/shard_map/reduce_scatter | solution.py:276
  1708.4 178.4 %reduce-scatter.9.cloned.1.call-done = f32[128,1024]{1,0:T(8,128)} async-done(((f32[2048,1024]{1,0:T(8,128)}), f32[128,1024]{1,0:T(8,128)}) %reduce-scatter.9.cloned.1.call-update) | async-done | bytes 524304 | tf_op jit(solution)/shard_map/reduce_scatter | solution.py:271
  1886.9 475.1 %reduce-scatter.11.cloned.1.call-done = f32[128,2816]{1,0:T(8,128)} async-done(((f32[2048,2816]{1,0:T(8,128)}), f32[128,2816]{1,0:T(8,128)}) %reduce-scatter.11.cloned.1.call-update) | async-done | bytes 1441808 | tf_op jit(solution)/shard_map/reduce_scatter | solution.py:274
  2362.0 475.9 %reduce-scatter.13.cloned.1.call-done = f32[128,2816]{1,0:T(8,128)} async-done(((f32[2048,2816]{1,0:T(8,128)}), f32[128,2816]{1,0:T(8,128)}) %reduce-scatter.13.cloned.1.call-update) | async-done | bytes 1441808 | tf_op jit(solution)/shard_map/reduce_scatter | solution.py:275
  2837.8 518.2 %reduce-scatter.7.cloned.1.call-done = f32[128,3,1024]{2,0,1:T(8,128)} async-done(((f32[2048,3,1024]{2,0,1:T(8,128)}), f32[128,3,1024]{2,0,1:T(8,128)}) %reduce-scatter.7.cloned.1.call-update) | async-done | bytes 1572880 | tf_op jit(solution)/shard_map/reduce_scatter | solution.py:269
  (363 shorter events, 443.2 us)
Async XLA Ops:
  7.2 182.8 %all-gather.6.cloned.1.call-start = ((), (), s32[]{:S(2)}) async-start(), calls=%async_computation.13 | async-start | bytes 14155776 | tf_op jit(solution)/shard_map/all_gather | solution.py:139
  10.1 191.3 %copy-start.30 = (f32[2048]{0:T(1024)}, f32[2048]{0:T(1024)S(1)}, u32[]{:S(2)}) copy-start(f32[2048]{0:T(1024)S(1)} %convert_element_type.243) | copy-start | bytes 24580
  10.2 191.3 %copy-start.20 = (f32[2048]{0:T(1024)}, f32[2048]{0:T(1024)S(1)}, u32[]{:S(2)}) copy-start(f32[2048]{0:T(1024)S(1)} %convert_element_type.242) | copy-start | bytes 24580
  10.6 190.9 %copy-start.25 = (f32[512]{0:T(512)}, f32[512]{0:T(512)S(1)}, u32[]{:S(2)}) copy-start(f32[512]{0:T(512)S(1)} %broadcast_multiply_fusion.5) | copy-start | bytes 6148
  12.0 199.3 %copy-start.18 = (f32[512,8]{0,1:T(8,128)}, f32[512,8]{0,1:T(8,128)S(1)}, u32[]{:S(2)}) copy-start(f32[512,8]{0,1:T(8,128)S(1)} %get-tuple-element.342) | copy-start | bytes 49156
  225.7 19.6 all-to-all-start
  245.3 21.2 all-to-all-start.1
  266.6 37.9 %all-to-all-start.2 = ((bf16[2,2,131072]{2,1,0:T(2,128)(2,1)}), bf16[2,2,131072]{2,1,0:T(2,128)(2,1)}, u32[]{:S(2)}, u32[]{:S(2)}) async-start(bf16[2,2,131072]{2,1,0:T(2,128)(2,1)} %reshape.587), calls=%async_computation.2 | async-start | bytes 2097152 | tf_op jit(solution)/shard_map/all_to_all | solution.py:166
  271.0 117.6 %all-gather.8.cloned.1.call-start = ((), (), s32[]{:S(2)}) async-start(), calls=%async_computation.14 | async-start | bytes 4718592 | tf_op jit(solution)/shard_map/all_gather | solution.py:140
  271.8 150.7 %all-reduce.11.cloned.1.call-start = ((), (), s32[]{:S(2)}) async-start(), calls=%async_computation.15 | async-start | bytes 8388608 | tf_op jit(solution)/shard_map/psum | solution.py:180
  395.6 194.0 %all-gather.10.cloned.1.call-start = ((), (), s32[]{:S(2)}) async-start(), calls=%async_computation.16 | async-start | bytes 12976128 | tf_op jit(solution)/shard_map/all_gather | solution.py:183
  396.2 357.5 %all-gather.12.cloned.1.call-start = ((), (), s32[]{:S(2)}) async-start(), calls=%async_computation.17 | async-start | bytes 12976128 | tf_op jit(solution)/shard_map/all_gather | solution.py:184
  396.8 521.1 %all-gather.14.cloned.1.call-start = ((), (), s32[]{:S(2)}) async-start(), calls=%async_computation.18 | async-start | bytes 12976128 | tf_op jit(solution)/shard_map/all_gather | solution.py:185
  397.3 576.5 %all-reduce.13.cloned.1.call-start = ((), (), s32[]{:S(2)}) async-start(), calls=%async_computation.19 | async-start | bytes 4194304 | tf_op jit(solution)/shard_map/psum | solution.py:214
  601.0 316.8 %copy-start.14 = (bf16[1,512,2048]{2,1,0:T(8,128)(2,1)S(1)}, bf16[1,512,2048]{2,1,0:T(8,128)(2,1)}, u32[]{:S(2)}) copy-start(bf16[1,512,2048]{2,1,0:T(8,128)(2,1)} %param.31) | copy-start | bytes 6291460
  1109.5 19.3 all-to-all-start.7
  1128.8 19.9 all-to-all-start.6
  1148.7 24.0 all-to-all-start.5
  1153.2 112.2 %all-reduce.15.cloned.1.call-start = ((), (), s32[]{:S(2)}) async-start(), calls=%async_computation.25 | async-start | bytes 8388608 | tf_op jit(solution)/shard_map/psum | solution.py:194
  1193.3 512.2 %reduce-scatter.15.cloned.1.call-start = ((), (), s32[]{:S(2)}) async-start(), calls=%async_computation.24 | async-start | bytes 24510464 | tf_op jit(solution)/shard_map/reduce_scatter | solution.py:276
  1209.3 677.5 %reduce-scatter.9.cloned.1.call-start = ((), (), s32[]{:S(2)}) async-start(), calls=%async_computation.21 | async-start | bytes 8912896 | tf_op jit(solution)/shard_map/reduce_scatter | solution.py:271
  1218.7 1143.3 %reduce-scatter.11.cloned.1.call-start = ((), (), s32[]{:S(2)}) async-start(), calls=%async_computation.22 | async-start | bytes 24510464 | tf_op jit(solution)/shard_map/reduce_scatter | solution.py:274
  1234.0 1603.9 %reduce-scatter.13.cloned.1.call-start = ((), (), s32[]{:S(2)}) async-start(), calls=%async_computation.23 | async-start | bytes 24510464 | tf_op jit(solution)/shard_map/reduce_scatter | solution.py:275
  1247.0 2109.1 %reduce-scatter.7.cloned.1.call-start = ((), (), s32[]{:S(2)}) async-start(), calls=%async_computation.20 | async-start | bytes 26738688 | tf_op jit(solution)/shard_map/reduce_scatter | solution.py:269
  (40 other events, 570.3 us)
Sparse Core Ops, SparseCore 0:
  10.7 179.2 all-gather.5
  274.0 72.0 all-gather.7
  395.7 26.6 all-reduce.10
  424.7 164.7 all-gather.9
  591.8 161.8 all-gather.11
  756.0 161.8 all-gather.13
  954.4 19.3 all-reduce.12
  1193.5 30.1 all-reduce.14
  1226.1 479.4 reduce-scatter.14
  1708.4 178.4 reduce-scatter.8
  1889.9 472.0 reduce-scatter.10
  2364.8 472.9 reduce-scatter.12
  2840.8 515.1 reduce-scatter.6
where the time goes:
time: 3370 us; the launch traced here: 3360 us
  waiting for transfers between devices  2670 us (79%)
  matrix products  263 us (8%)
  blocking collectives  140 us (4%)
  local copies, waits for them, and re-layouts  137 us (4%)
  other arithmetic  108 us (3%)
    reduce_scatter x1, waiting for transfers between devices, shards(): lax.psum_scatter(d_qkv_w, ('fsdp', 'ctx'), scatter_dimension=0, tiled=True)  518 us
    reduce_scatter x1, waiting for transfers between devices, shards(): lax.psum_scatter(d_up_w, ('fsdp', 'ctx'), scatter_dimension=0, tiled=True)  476 us
    reduce_scatter x1, waiting for transfers between devices, shards(): lax.psum_scatter(d_gate_w, ('fsdp', 'ctx'), scatter_dimension=0, tiled=True)  475 us
    reduce_scatter x1, waiting for transfers between devices, shards(): lax.psum_scatter(d_down, ('fsdp', 'ctx'), scatter_dimension=0, tiled=True)  332 us
    reduce_scatter x1, waiting for transfers between devices, shards(): lax.psum_scatter(d_out_w, ('fsdp', 'ctx'), scatter_dimension=0, tiled=True)  178 us
    all_gather x1, waiting for transfers between devices, shards(): lax.all_gather(qkv_weight, 'fsdp', axis=0, tiled=True)  178 us
    all_gather x1, waiting for transfers between devices, shards(): lax.all_gather(gate_weight, 'fsdp', axis=0, tiled=True)  162 us
    all_gather x1, waiting for transfers between devices, shards(): lax.all_gather(up_weight, 'fsdp', axis=0, tiled=True)  153 us
  transfers between devices with their start and end apart: 19, of which 11 were waited for; matrix products, arithmetic and copies ran while one was open for 8% of the time, Pallas kernels for 0%

commit v1 on v0

v1 whole, which is shorter than its diff:
```python
import heapq
import math

import jax
import jax.numpy as jnp
from jax import lax
from jax.experimental import pallas as pl
from jax.experimental.pallas import tpu as pltpu
from jax.sharding import PartitionSpec as P

ROT = 16
EPSILON = 1e-05
THETA = 10000.0
MASKED = -1e30
F32 = jnp.float32
BF16 = jnp.bfloat16
ANY = pl.BlockSpec(memory_space=pl.ANY)
VMEM = pl.BlockSpec(memory_space=pltpu.VMEM)
MESH = pl.DeviceIdType.MESH
LINK = 0.085e6
CHIP = 0.5e6
ROWS = 256
PLAN = {
    "forward_kernel": {
        (0, 1): 10.3, (1, 1): 10.9, (2, 1): 10.3, (4, 2): 57.0, (5, 3): 65.6, (6, 4): 140.0, (7, 4): 140.0,
        (8, 2): 14.5, (8, 3): 34.2, (8, 4): 54.4, (8, 5): 43.9, (9, 3): 31.0, (9, 4): 47.0, (9, 5): 66.1,
        (9, 6): 68.6, (10, 3): 35.5, (10, 4): 53.6, (10, 5): 78.9, (10, 6): 87.3, (11, 3): 74.9, (11, 4): 100.3,
        (11, 5): 111.3, (11, 6): 115.3, (12, 3): 93.8, (12, 4): 127.7, (12, 5): 167.3, (12, 6): 170.8, (13, 3): 176.4,
        (13, 4): 205.9, (13, 5): 227.9, (13, 6): 231.8, (14, 3): 185.1, (14, 4): 228.6, (14, 5): 248.6,
        (14, 6): 241.0, (15, 1): 4.8, (16, 2): 20.1, (16, 3): 28.2, (17, 2): 41.5, (17, 3): 78.0, (18, 1): 4.6,
        (18, 3): 10.5, (18, 5): 10.5, (20, 2): 45.8, (21, 2): 70.4, (22, 2): 89.1, (23, 2): 117.7, (24, 2): 103.7,
        (24, 3): 160.8, (25, 3): 173.0, (25, 5): 177.9, (25, 7): 182.6, (25, 9): 187.0, (25, 10): 190.8,
        (26, 31): 109.2, (27, 3): 163.5, (27, 4): 185.3, (28, 2): 195.6, (29, 2): 217.5, (29, 3): 230.7,
    },
    "feed_kernel": {
        (0, 3): 2.7, (0, 14): 78.4, (0, 16): 73.7, (1, 3): 39.6, (1, 4): 59.9, (2, 1): 89.7, (2, 2): 72.2,
        (3, 2): 107.6, (3, 3): 129.7, (4, 2): 51.9, (4, 3): 67.3, (4, 4): 85.0, (4, 5): 107.7, (4, 6): 113.7,
        (5, 2): 71.5, (5, 3): 89.0, (5, 4): 107.8, (5, 5): 113.6, (5, 6): 137.8,
    },
    "attend_back_kernel": {
        (0, 1): 0.2, (0, 2): 16.8, (0, 3): 42.3, (0, 4): 65.5, (0, 5): 79.3, (1, 2): 10.9, (1, 3): 30.6, (1, 4): 51.4,
        (1, 5): 79.0, (1, 6): 84.9, (2, 2): 18.0, (2, 3): 46.1, (2, 4): 73.6, (2, 5): 82.7, (2, 6): 97.0, (3, 1): 2.7,
        (3, 2): 47.3, (3, 3): 65.4, (4, 2): 30.7, (4, 3): 42.2, (5, 0): 2.7, (5, 22): 0.0, (5, 25): 78.2,
    },
    "last_kernel": {
        (0, 1): 2.7, (1, 1): 12.1, (2, 2): 25.8, (2, 3): 45.0, (3, 1): 2.7, (3, 2): 56.6, (4, 2): 58.4, (4, 3): 67.9,
        (4, 4): 64.3, (4, 5): 80.0, (5, 1): 4.4, (5, 2): 19.7, (5, 3): 51.1, (5, 4): 95.6, (5, 5): 105.8,
        (6, 2): 11.4, (6, 3): 26.5, (6, 4): 54.3, (6, 5): 85.5, (6, 6): 97.6, (7, 3): 23.7, (7, 4): 37.7,
        (7, 5): 79.2, (7, 6): 98.1, (7, 7): 110.3, (8, 3): 16.9, (8, 4): 53.1, (8, 5): 85.3, (8, 6): 100.1,
        (8, 7): 112.8, (9, 3): 31.2, (9, 4): 64.5, (9, 5): 97.7, (9, 6): 103.3, (9, 7): 114.8,
    },
}
GRAD_AFTER = 4
NEAR_LATE = 5
EARLY = (0, 0, 1, 0, 0, 0, 0)
SLACK = (0.0, 0.0, 0.0, 10.0, 10.0, 10.0, 5.0)


def mm(left, right):
    return jnp.dot(left, right, preferred_element_type=F32)


def mm_nt(left, right):
    return lax.dot_general(left, right, (((1,), (1,)), ((), ())), preferred_element_type=F32)


def mm_tn(left, right):
    return lax.dot_general(left, right, (((0,), (0,)), ((), ())), preferred_element_type=F32)


def shape(dims, dtype):
    return jax.ShapeDtypeStruct(tuple(dims), dtype)


def nbytes(ref):
    return math.prod(ref.shape) * jnp.dtype(ref.dtype).itemsize


class Event:
    def __init__(self):
        self.done = False
        self.waiters = []


class Copy:
    def __init__(self, kern, src, dst, to, into):
        self.kern = kern
        self.send_sem = kern.sem()
        self.recv_sem = kern.sem()
        self.desc = pltpu.make_async_remote_copy(src, dst, self.send_sem, self.recv_sem, device_id=to, device_id_type=MESH)
        into = dst if into is None else into
        self.arrival = pltpu.make_async_remote_copy(
            into, into, self.send_sem, self.recv_sem, device_id=to, device_id_type=MESH
        )

    def start(self, cond=None, late=True):
        self.cond = cond
        run_if(cond, self.desc.start)
        if late:
            self.kern.sent.append((cond, self.desc.wait_send))

    def gone(self):
        run_if(self.cond, self.desc.wait_send)

    def wait(self, cond=None):
        run_if(cond, self.arrival.wait_recv)


def run_if(cond, step):
    if cond is None:
        step()
    else:
        pl.when(cond)(lambda: step())


class Kern:
    def __init__(self, line, sems, name):
        self.line = line
        self.sems = sems
        self.used = 0
        self.sent = []
        self.now = 0.0
        self.queue = []
        self.count = 0
        self.busy = {}
        self.ended = []
        self.plan = PLAN.get(name, {}) if line == 4 else {}
        fsdp = lax.axis_index("fsdp")
        self.z = fsdp // 2
        self.x = lax.rem(fsdp, 2)
        self.y = lax.axis_index("ctx")
        self.c = lax.axis_index("tp")
        self.home = self.c == self.x
        self.away = self.c != self.x
        self.q = self.x * 2 + self.y
        self.nx = (self.z * 2 + 1 - self.x, self.y, self.c)
        self.ny = (fsdp, 1 - self.y, self.c)
        self.diag = (self.z * 2 + 1 - self.x, 1 - self.y, self.c)
        self.sib = (fsdp, self.y, 1 - self.c)
        self.has_up = self.z < line - 1
        self.has_dn = self.z > 0
        self.up = self.at_line(1)
        self.dn = self.at_line(-1)

    def segment(self, name, step):
        pass

    def sem(self):
        self.used += 1
        return self.sems.at[self.used - 1]

    def at_line(self, shift):
        n = self.line
        return (lax.rem(self.z + shift + n, n) * 2 + self.x, self.y, self.c)

    def greet(self):
        barrier = pltpu.get_barrier_semaphore()
        peers = 3 + self.line
        for to in (self.nx, self.ny, self.diag, self.sib):
            pl.semaphore_signal(barrier, inc=1, device_id=to, device_id_type=MESH)
        for d in range(1, self.line):
            pl.semaphore_signal(barrier, inc=1, device_id=self.at_line(d), device_id_type=MESH)
        pl.semaphore_wait(barrier, peers)

    def remote(self, src, dst, to, into=None):
        return Copy(self, src, dst, to, into)

    def local(self, src, dst):
        return pltpu.make_async_copy(src, dst, self.sem())

    def link(self, name, size, rate):
        end = max(self.now, self.busy.get(name, 0.0)) + size / rate
        self.busy[name] = end
        return end + 1.0

    def add(self, task, at=0.0):
        self.count += 1
        heapq.heappush(self.queue, (at, self.count, task))

    def fire(self, event):
        event.done = True
        for task in event.waiters:
            self.add(task, self.now)

    def run(self):
        steps = {}
        while self.queue:
            at, _, task = heapq.heappop(self.queue)
            self.now = max(self.now, at)
            while True:
                name, step = steps.setdefault(id(task), (len(steps), 0))
                steps[id(task)] = (name, step + 1)
                self.segment(name, step)
                try:
                    want = next(task)
                except StopIteration:
                    self.ended.append(task)
                    break
                if not isinstance(want, Event):
                    want = self.plan.get((name, step + 1), want)
                if isinstance(want, Event):
                    if want.done:
                        continue
                    want.waiters.append(task)
                    break
                self.add(task, want)
                break
        for cond, wait in self.sent:
            run_if(cond, wait)


def call(body, ins, outs, scratch, line, cid, sems, vmem_mb, name, flops=0):
    def run(*refs):
        kern = Kern(line, refs[-1], name)
        kern.greet()
        body(kern, refs[: len(ins)], refs[len(ins) : len(ins) + len(outs)], refs[len(ins) + len(outs) : -1])
        kern.run()
        assert kern.used <= sems, kern.used

    return pl.pallas_call(
        run,
        out_shape=[out for out, _ in outs],
        in_specs=[spec for _, spec in ins],
        out_specs=[spec for _, spec in outs],
        scratch_shapes=list(scratch) + [pltpu.SemaphoreType.DMA((sems,))],
        compiler_params=pltpu.CompilerParams(
            collective_id=cid, has_side_effects=True, vmem_limit_bytes=vmem_mb * 1024 * 1024
        ),
        name=name,
    )(*[array for array, _ in ins])


def rows_loop(total, step, body):
    @pl.loop(0, total // step)
    def _(index):
        body(pl.ds(pl.multiple_of(index * step, step), step))


def store_rows(target, lead, i, value, rows):
    chunk, cols = value.shape
    count = chunk // rows
    if count <= 4:
        share = 4 // count
        target[lead + (i // share, pl.ds(lax.rem(i, share) * count, count))] = value.reshape(count, rows, cols)
    else:
        target[lead + (pl.ds(i * (count // 4), count // 4),)] = value.reshape(count // 4, 4, rows, cols)


def plane_gather(k, own, full, ready=None, sent=None, done=None, slack=0.0):
    if ready is not None:
        yield ready
    tokens = own.shape[0]
    size = nbytes(own) / 2
    a, b = pl.ds(0, tokens // 2), pl.ds(tokens // 2, tokens // 2)
    y, o = k.y, 1 - k.y
    keep = k.local(own, full.at[y])
    x_a = k.remote(own.at[a], full.at[y, a], k.nx)
    y_b = k.remote(own.at[b], full.at[y, b], k.ny, into=full.at[o, b])
    x_b = k.remote(own.at[b], full.at[y, b], k.nx)
    y_a = k.remote(own.at[a], full.at[y, a], k.ny, into=full.at[o, a])
    pass_y = k.remote(full.at[y, a], full.at[y, a], k.ny, into=full.at[o, a])
    pass_x = k.remote(full.at[o, b], full.at[o, b], k.nx)
    for copy in (x_a, y_b, x_b, y_a):
        copy.start(k.home)
    pl.when(k.home)(keep.start)
    k.link("x", size, LINK)
    yield k.link("y", size, LINK) + slack
    x_a.wait(k.away)
    pass_y.start(k.away)
    y_b.wait(k.home)
    pass_x.start(k.home)
    if sent is not None:
        k.fire(sent)
    k.link("x", 2 * size, LINK)
    yield k.link("y", 2 * size, LINK) + slack
    x_b.wait(k.away)
    y_a.wait(k.home)
    pass_y.wait(k.away)
    pass_x.wait(k.away)
    pl.when(k.home)(keep.wait)
    if done is not None:
        k.fire(done)


def plane_scatter(k, part, got, sx, sy, far=None, ready=None, done=None):
    if far is not None:
        yield far
    half = part.shape[1] // 2
    size = nbytes(part) / 4
    a, b = pl.ds(0, half), pl.ds(half, half)
    y, o = k.y, 1 - k.y
    y_far = k.remote(part.at[o, a], got, k.ny)
    x_far = k.remote(part.at[o, b], got, k.nx)
    y_a = k.remote(part.at[o, a], sy.at[a], k.ny)
    x_b = k.remote(part.at[y, b], sx.at[b], k.nx)
    x_a = k.remote(part.at[y, a], sx.at[a], k.nx)
    y_b = k.remote(part.at[o, b], sy.at[b], k.ny)
    y_far.start(k.away)
    x_far.start(k.away)
    y_a.start(k.home)
    k.link("x", 2 * size, LINK)
    when = k.link("y", 2 * size, LINK)
    if ready is not None:
        yield ready
    x_b.start(k.away)
    yield when
    y_far.wait(k.away)
    x_far.wait(k.home)
    index = jnp.where(k.home, o, y)
    first = jnp.where(k.home, half, 0)

    @pl.loop(0, half // 32)
    def _(i):
        at = pl.ds(pl.multiple_of(first + i * 32, 32), 32)
        more = got[pl.ds(pl.multiple_of(i * 32, 32), 32), :]
        part[index, at, :] = (part[index, at, :].astype(F32) + more.astype(F32)).astype(BF16)

    k.now += 1.0
    x_a.start(k.away)
    y_b.start(k.home)
    k.link("x", size, LINK)
    yield k.link("y", size, LINK)
    x_b.wait(k.home)
    x_a.wait(k.home)
    y_a.wait(k.home)
    y_b.wait(k.home)
    if done is not None:
        k.fire(done)


def scatter_scratch(tokens, width):
    return [
        pltpu.VMEM((tokens // 2, width), BF16),
        pltpu.VMEM((tokens, width), BF16),
        pltpu.VMEM((tokens, width), BF16),
    ]


def scatter_sum(k, part, sx, sy, at):
    return part[k.y, at, :].astype(F32) + sx[at, :].astype(F32) + sy[at, :].astype(F32)


def near_gather(k, source, block, event):
    own = source(k.q)
    near = k.remote(source((1 - k.x) * 2 + k.y), block(0, k.z, k.x), k.nx, into=block(0, k.z, 1 - k.x))
    keep = k.local(own, block(0, k.z, k.x))
    near.start()
    keep.start()
    yield k.link("x", nbytes(own) * 2, LINK)
    near.wait()
    keep.wait()
    k.fire(event)


def line_gather(k, pair, size, ready=(), early=0, following=None, done=None, slack=0.0, first=None):
    n = k.line
    z = k.z

    def at_line(shift):
        return lax.rem(z + shift + n, n)

    def send(src, spot, arrival, to, ok):
        copy = k.remote(src, spot, to, into=arrival)
        copy.start(ok)
        return copy

    heads = []
    if first is not None and n > 1:
        own, block = first
        heads.append(
            (
                send(own, block(0, z, k.x), block(0, at_line(-1), k.x), k.up, k.has_up),
                send(own, block(0, z, k.x), block(0, at_line(1), k.x), k.dn, k.has_dn),
            )
        )
    for event in ready:
        yield event

    hop = size / LINK
    end = k.link("z", size * (n - 1), LINK) if n > 1 else k.now + 1.0
    across = []
    moving = None
    for d in range(n):
        if d:
            yield max(k.now, end - (n - 1 - d) * hop) + slack
        up_ok, dn_ok = z >= d, z + d < n
        left, right = at_line(-d), at_line(d)
        if d:
            for up, dn in moving:
                up.wait(up_ok)
                dn.wait(dn_ok)
        if d == 0 and heads:
            near = first[1](0, z, 1 - k.x)
            heads.append(
                (
                    send(near, near, first[1](0, at_line(-1), 1 - k.x), k.up, k.has_up),
                    send(near, near, first[1](0, at_line(1), 1 - k.x), k.dn, k.has_dn),
                )
            )
            moving = heads
        elif d < n - 1:
            up = send(pair(0, left), pair(0, left), pair(0, at_line(-d - 1)), k.up, up_ok & k.has_up)
            dn = send(pair(0, right), pair(0, right), pair(0, at_line(d + 1)), k.dn, dn_ok & k.has_dn)
            moving = [(up, dn)]
        if d == min(early, n - 1) and following is not None:
            k.fire(following)
        for index, ok in ((left, up_ok), (right, dn_ok)) if d else ((z, None),):
            copy = k.remote(pair(0, index), pair(1, index), k.sib)
            copy.start(ok)
            across.append((copy, ok))
    yield k.now + size / 2 / CHIP + 1.0
    for copy, ok in across:
        copy.wait(ok)
    if done is not None:
        k.fire(done)


def line_scatter(
    k, own, sib_part, sibling, from_dn, from_up, got, rows=None, own_part=None, ready=(), following=None, done=None, early=0, slack=0.0
):
    for event in ready:
        yield event
    n = k.line
    z = k.z
    first, count = rows or (0, own.shape[2])
    part = pl.ds(first, count)
    size = nbytes(own) * 2 / n * count / own.shape[2]
    hop = size / LINK
    step = min(count, 64)
    spot = [lax.rem(z + d, n) for d in range(n)]
    order = []
    for d in range(n - 1, 0, -1):
        for e in (d, n - d):
            if e not in order:
                order.append(e)
    order.append(0)
    loads, crosses = {}, {}
    for d in order:
        if own_part is not None:
            loads[d] = k.local(own_part.at[spot[d], :, part], own.at[spot[d], :, part])
            loads[d].start()
        crosses[d] = k.remote(sib_part.at[spot[d], :, part], sibling.at[spot[d], :, part], k.sib)
        crosses[d].start()

    def plus(index, source):
        for quarter in range(4):

            def add(at):
                at = pl.ds(pl.multiple_of(first + at.start, 16), at.size)
                more = source(quarter, at)
                own[index, quarter, at, :] = (own[index, quarter, at, :].astype(F32) + more.astype(F32)).astype(BF16)

            rows_loop(count, step, add)

    def prepare(d):
        if d in loads:
            loads[d].wait()
        crosses[d].wait()
        plus(spot[d], lambda quarter, at: sibling[spot[d], quarter, at, :])
        k.now += size / 2.0e6

    def take(d, source, index, cond):
        pl.when(cond)(lambda: plus(index, lambda quarter, at: source[d, quarter, at, :]))
        k.now += size / 2.0e6

    yield k.link("c", size * n / 2, CHIP)
    up = down = None
    end = k.link("z", size * (n - 1), LINK) if n > 1 else k.now
    for d in range(n - 1, -1, -1):
        for e in (d, n - d):
            if e in order:
                prepare(e)
                order.remove(e)
        up_ok, dn_ok = (z >= 1) & (z + d < n), (z <= n - 2) & (z >= d)
        if d < n - 1:
            up.wait(up_ok)
            take(d, from_dn, spot[d], up_ok)
        if d:
            after = k.remote(own.at[spot[d], :, part], from_dn.at[d - 1, :, part], k.up)
            if up is not None:
                up.gone()
            after.start((z + d < n) & k.has_up, late=False)
            up = after
        if d < n - 1:
            down.wait(dn_ok)
            take(d, from_up, spot[(n - d) % n], dn_ok)
        if d:
            after = k.remote(own.at[spot[n - d], :, part], from_up.at[d - 1, :, part], k.dn)
            if down is not None:
                down.gone()
            after.start((z >= d) & k.has_dn, late=False)
            down = after
        if d == n - 1 - early and following is not None:
            k.fire(following)
        if d:
            yield max(k.now, end - (d - 1) * hop) + slack
    for copy in (up, down):
        if copy is not None:
            copy.gone()
    yield from quarters_exchange(k, own.at[z, :, part], got.at[:, part])
    if done is not None:
        k.fire(done)


def quarters_exchange(k, block, got):
    keep = k.local(block.at[k.q], got.at[k.q])
    keep.start()
    copies = []
    for away, to in ((3, k.diag), (2, k.nx), (1, k.ny)):
        other = (1 - k.x if away & 2 else k.x) * 2 + (1 - k.y if away & 1 else k.y)
        copy = k.remote(block.at[other], got.at[k.q], to, into=got.at[other])
        copy.start()
        copies.append(copy)
    size = nbytes(got) / 2
    k.link("x", size, LINK)
    yield k.link("y", size, LINK)
    for copy in copies:
        copy.wait()
    keep.wait()


def line_scratch(line, rows, cols):
    more = max(line - 1, 1)
    return [pltpu.VMEM((line, 4, rows, cols), BF16)] + [pltpu.VMEM((more, 4, rows, cols), BF16) for _ in range(2)]


def line_sems(line):
    return 14 * line + 20


def norm_rows(source):
    average = jnp.mean(source, axis=-1, keepdims=True)
    centered = source - average
    inv_std = lax.rsqrt(jnp.mean(centered * centered, axis=-1, keepdims=True) + EPSILON)
    return centered * inv_std, inv_std


def norm_back(gradient, scaled, inv_std, gain_vec):
    inner = gradient * gain_vec
    return inv_std * (
        inner - jnp.mean(inner, axis=-1, keepdims=True) - scaled * jnp.mean(inner * scaled, axis=-1, keepdims=True)
    )


def fold(rows):
    return rows[:8] + rows[8:]


def head_mask(rows, side, dtype):
    lane = lax.broadcasted_iota(jnp.int32, (rows, 128), 1)
    return (lane // 64 == side).astype(dtype)


def turn_lanes(value, cosine, sine_a, sine_b):
    return value * cosine + pltpu.roll(value, 120, 1) * sine_a + pltpu.roll(value, 8, 1) * sine_b


def expand_tables(tables, cosine, sine_a, sine_b):
    tokens = tables.shape[1]
    lane = lax.broadcasted_iota(jnp.int32, (128, 128), 1)
    spot = lax.rem(lane, 64)
    for half in range(2):

        def step(at):
            value = tables[half, at, :]
            other = pltpu.roll(value, 64, 1)
            sine = jnp.where(lane < 64, other, value)
            full = pl.ds(pl.multiple_of(half * tokens + at.start, 128), 128)
            cosine[full, :] = jnp.where(spot < 16, jnp.where(lane < 64, value, other), 1.0)
            sine_a[full, :] = jnp.where(spot < 8, -sine, 0.0)
            sine_b[full, :] = jnp.where((spot >= 8) & (spot < 16), sine, 0.0)

        rows_loop(tokens, 128, step)


def mark_documents(tables, key_marks, query_marks):
    tokens = tables.shape[1]
    lane = lax.broadcasted_iota(jnp.int32, (128, 128), 1)
    for half in range(2):

        def step(at):
            segment = tables[half, at, 32:33].astype(jnp.int32)
            full = pl.ds(pl.multiple_of(half * tokens + at.start, 128), 128)
            for side in range(2):
                document = lane - (1 - side) * 64
                same = document == segment
                used = (document >= 0) & (document < 4)
                key_marks[side, full, :] = jnp.where(same, 1.0, 0.0).astype(BF16)
                query_marks[side, full, :] = jnp.where(used & jnp.logical_not(same), MASKED, 0.0).astype(BF16)

        rows_loop(tokens, 128, step)


BLOCK = 256


def causal(scores):
    key = lax.broadcasted_iota(jnp.int32, scores.shape, 0)
    query = lax.broadcasted_iota(jnp.int32, scores.shape, 1)
    return jnp.where(key <= query, scores, MASKED)


def mark_keys(k_ref, pair, key_marks, marked):
    length = k_ref.shape[1]
    for side in range(2):
        marked[side] = k_ref[pair] * head_mask(length, side, BF16) + key_marks[side]


def attention_forward(k, q_ref, v_ref, marked, query_marks, out_ref, out_t, lse_ref, pair, out_lanes):
    length = q_ref.shape[1]
    v_t = v_ref[pair].astype(F32).T.astype(BF16)
    for i in range(length // BLOCK):
        low, extent = i * BLOCK, (i + 1) * BLOCK
        at = slice(low, extent)
        sides = []
        for side in range(2):
            queries = q_ref[pair, at, :] * head_mask(BLOCK, side, BF16) + query_marks[side, at, :]
            scores = [causal(mm_nt(marked[side, at, :], queries))]
            if i:
                scores.append(mm_nt(marked[side, :low, :], queries))
            tops = [jnp.max(part, axis=0, keepdims=True) for part in scores]
            top = jnp.maximum(tops[0], tops[1]) if i else tops[0]
            weights = [jnp.exp(part - top) for part in scores]
            total = sum(jnp.sum(part, axis=0, keepdims=True) for part in weights)
            rows = slice(side * 64, side * 64 + 64)
            value = mm(v_t[rows, at], weights[0].astype(BF16))
            if i:
                value = value + mm(v_t[rows, :low], weights[1].astype(BF16))
            sides.append(value * (1.0 / total))
            lse_ref[pair, side : side + 1, at] = top + jnp.log(total)
        both = jnp.concatenate(sides, axis=0)
        out_t[pair, :, at] = both
        out_ref[at, out_lanes] = both.T.astype(BF16)
        k.now += 0.5 + 0.3 * i
        yield k.now


def attention_backward(k, q_ref, v_ref, marked, query_marks, out_t, lse_ref, do_ref, dq_t, dk, dv, k_ref, pair):
    length = q_ref.shape[1]
    k_t = k_ref[pair].astype(F32).T.astype(BF16)
    inner = do_ref[pair].astype(F32).T * out_t[pair]
    inner = [jnp.sum(inner[side * 64 : side * 64 + 64], axis=0, keepdims=True) for side in range(2)]
    for i in range(length // BLOCK):
        at = slice(i * BLOCK, (i + 1) * BLOCK)
        for side in range(2):
            mask = head_mask(BLOCK, side, BF16)
            plain = q_ref[pair, at, :] * mask
            queries = plain + query_marks[side, at, :]
            grads = do_ref[pair, at, :] * mask
            lse = lse_ref[pair, side : side + 1, at]
            turned = None
            for j in range(i, -1, -1):
                of = slice(j * BLOCK, (j + 1) * BLOCK)
                scores = mm_nt(marked[side, of, :], queries)
                if j == i:
                    scores = causal(scores)
                probability = jnp.exp(scores - lse)
                d_prob = mm_nt(v_ref[pair, of, :], grads)
                d_scores = (probability * (d_prob - inner[side][:, at])).astype(BF16)
                part_v = mm(probability.astype(BF16), grads)
                part_k = mm(d_scores, plain)
                if j == i and side == 0:
                    dv[of, :] = part_v
                    dk[of, :] = part_k
                else:
                    dv[of, :] += part_v
                    dk[of, :] += part_k
                part_q = mm(k_t[side * 64 : side * 64 + 64, of], d_scores)
                turned = part_q if turned is None else turned + part_q
            dq_t[side * 64 : side * 64 + 64, at] = turned
        k.now += 1.0 + 0.8 * i
        yield k.now


def forward_kernel(line, x, gains, grad, table, bias, qkv, out_w, gate, up, down):
    tokens, width = x.shape
    length = 2 * tokens
    rows = width // (2 * line)
    cols_q = out_w.shape[1] // 4
    ff = gate.shape[1]
    ff_q = ff // 4
    pairs = cols_q // 64

    def body(k, ins, outs, scratch):
        x, gains, grad, table, bias, qkv, out_w, gate, up, down = ins
        h_out, g_out, h2_out, resid, w_qkv, w_out, w_gate, w_up, w_down = outs[:9]
        q_out, key_out, v_out, o_out, o_t_out, lse, tables, d_hid_out = outs[9:]
        h_own, h_full, b_full, wq, wo, whole, pieces, cosine, sine_a, sine_b, key_marks, query_marks, marked, part, got, sx, sy, r_own, h2_own = scratch[:-8]
        q, key, v, o, o_t, g_full, w_d, d_hid = scratch[-8:]
        h_there, t_there, b_there, g_there = (Event() for _ in range(4))
        loaded_out, far, parted, summed, h2_ready = (Event() for _ in range(5))
        loaded_qkv = [Event() for _ in range(3)]
        cut = [Event() for _ in range(3)]
        h_sent, g_sent = Event(), Event()

        def norm_one():
            @pl.when(k.home)
            def _():
                def step(at):
                    scaled, _ = norm_rows(x[at, :].astype(F32))
                    h_own[at, :] = (scaled * gains[0:1, :] + gains[1:2, :]).astype(BF16)

                rows_loop(tokens, 16, step)

            k.now += 3.0
            yield k.now

        def share_bias():
            copy = k.remote(bias, b_full.at[1], k.sib)
            copy.start()
            b_full[0] = bias[...]
            yield k.now + 3.0
            copy.wait()
            k.fire(b_there)

        def cut_quarters():
            weight = whole
            for i in (2, 0, 1):
                load = k.local((gate, up, down)[i], whole)
                load.start()
                yield k.now + 1.5
                load.wait()
                for quarter in range(4):
                    low = quarter * ff_q
                    base = low // 128 * 128
                    top = min(-(-(low + ff_q) // 128) * 128, ff)

                    for half in range(2):

                        def step(at):
                            full = pl.ds(pl.multiple_of(half * (rows // 2) + at.start, 16), 16)
                            value = weight[full, base:top].astype(F32)
                            if low != base:
                                value = pltpu.roll(value, value.shape[1] - (low - base), 1)
                            pieces[i, quarter, half, at, :] = value[:, :ff_q].astype(BF16)

                        rows_loop(rows // 2, 16, step)
                k.now += 1.5
                k.fire(cut[i])
                yield k.now

        def prepare():
            yield t_there
            expand_tables(tables, cosine, sine_a, sine_b)
            mark_documents(tables, key_marks, query_marks)
            k.now += 2.0
            yield k.now

        def fetch(source, target, event, ready):
            yield event
            copy = k.local(source, target)
            copy.start()
            yield k.now + nbytes(target) / 3.0e6 + 1.0
            copy.wait()
            k.fire(ready)

        def work():
            yield h_there
            store = k.local(h_full, h_out)
            store.start()
            yield b_there

            def project(j, slot, half, at):
                full = pl.ds(pl.multiple_of(half * tokens + at.start, 256), at.size)
                value = mm(h_full[half, at, :], wq[slot, j].reshape(width, cols_q)) + b_full[slot, j : j + 1, :]
                for pp in range(cols_q // 128):
                    piece = value[:, pp * 128 : pp * 128 + 128]
                    if j < 2:
                        piece = turn_lanes(piece, cosine[full, :], sine_a[full, :], sine_b[full, :])
                    if j == 0:
                        piece = piece * 0.125
                    (q, key, v)[j][slot * 2 + pp, full, :] = piece.astype(BF16)

            for j in range(3):
                yield loaded_qkv[j]
                for slot in range(2):
                    for half in range(2):
                        rows_loop(tokens, 512, lambda at: project(j, slot, half, at))
                    k.now += 1.5
                    yield k.now
            for slot in range(2):
                for pp in range(cols_q // 128):
                    pair = slot * 2 + pp
                    mark_keys(key, pair, key_marks, marked)
                    lanes = slice(pp * 128, pp * 128 + 128)
                    yield from attention_forward(k, q, v, marked, query_marks, o.at[slot], o_t, lse, pair, lanes)
            stores = [store] + [
                k.local(source, target)
                for source, target in ((q, q_out), (key, key_out), (v, v_out), (o, o_out), (o_t, o_t_out))
            ]
            for copy in stores[1:]:
                copy.start()
            yield loaded_out
            for half, event in ((1 - k.y, far), (k.y, parted)):

                def close(at):
                    full = pl.ds(pl.multiple_of(half * tokens + at.start, 256), at.size)
                    value = sum(mm_nt(o[slot, full, :], wo[slot].reshape(width, cols_q)) for slot in range(2))
                    part[half, at, :] = value.astype(BF16)

                rows_loop(tokens, 512, close)
                k.now += 2.0
                k.fire(event)
                yield k.now
            yield k.now + 5.0
            for copy in stores:
                copy.wait()

        def hidden_back():
            yield g_there
            yield streamed[4]
            stores = []
            for side in range(2):
                load = k.local(w_down.at[side], w_d)
                load.start()
                for half in range(2):
                    fetch = k.local(g_out.at[half], g_full)
                    fetch.start()
                    yield k.now + 2.0
                    if half == 0:
                        load.wait()
                    fetch.wait()
                    if len(stores) >= 2:
                        stores[-2].wait()
                    d_hid[half] = mm(g_full[...], w_d[...].reshape(width, ff_q)).astype(BF16)
                    k.now += 2.5
                    stores.append(k.local(d_hid.at[half], d_hid_out.at[side, half]))
                    stores[-1].start()
                    yield k.now
            for store in stores[-2:]:
                store.wait()

        def norm_two():
            yield summed

            @pl.when(k.home)
            def _():
                def step(at):
                    value = x[at, :].astype(F32) + scatter_sum(k, part, sx, sy, at)
                    r_own[at, :] = value
                    scaled, _ = norm_rows(value)
                    h2_own[at, :] = (scaled * gains[2:3, :] + gains[3:4, :]).astype(BF16)

                rows_loop(tokens, 16, step)

            k.now += 4.0
            k.fire(h2_ready)
            keep = k.local(r_own, resid)
            pl.when(k.home)(keep.start)
            yield k.now + 20.0
            pl.when(k.home)(keep.wait)

        def columns(q):
            return pl.ds(pl.multiple_of(q * cols_q, cols_q), cols_q)

        units = []
        for j in range(3):
            units.append(
                (
                    lambda q, j=j: qkv.at[j, :, columns(q)],
                    lambda slot, z, x, j=j: w_qkv.at[slot, j, z, x],
                    lambda slot, z, j=j: w_qkv.at[slot, j, z],
                )
            )
        units.append(
            (lambda q: out_w.at[:, columns(q)], lambda slot, z, x: w_out.at[slot, z, x], lambda slot, z: w_out.at[slot, z])
        )
        for i, target in ((2, w_down), (0, w_gate), (1, w_up)):
            units.append(
                (
                    lambda q, i=i: pieces.at[i, q],
                    lambda slot, z, x, target=target: target.at[slot, z, pl.ds(2 * x, 2)],
                    lambda slot, z, target=target: target.at[slot, z],
                )
            )
        nears = [Event() for _ in units]
        going = [Event() for _ in units]
        streamed = [Event() for _ in units]

        def near_of(i):
            if i >= 3:
                yield h_sent
            if i >= NEAR_LATE:
                yield g_sent
            if i >= 4:
                yield cut[(2, 0, 1)[i - 4]]
            yield from near_gather(k, units[i][0], units[i][1], nears[i])

        for i in range(3):
            k.add(near_of(i))
        k.add(norm_one())
        for i in range(3, len(units)):
            k.add(near_of(i))
        for i, (source, block, pair) in enumerate(units):
            ready = (nears[i],) + ((going[i - 1],) if i else ())
            k.add(
                line_gather(
                    k,
                    pair,
                    nbytes(source(0)) * 4,
                    ready=ready,
                    early=EARLY[i],
                    following=going[i],
                    done=streamed[i],
                    slack=SLACK[i],
                    first=(source(k.q), block) if i < 3 else None,
                )
            )
        k.add(share_bias())
        k.add(plane_gather(k, table, tables, ready=nears[2], done=t_there))
        k.add(plane_gather(k, h_own, h_full, ready=nears[2], sent=h_sent, done=h_there))
        k.add(cut_quarters())
        k.add(prepare())
        for j in range(3):
            k.add(fetch(w_qkv.at[:, j], wq.at[:, j], streamed[j], loaded_qkv[j]))
        k.add(fetch(w_out, wo, streamed[3], loaded_out))
        k.add(plane_gather(k, grad, g_out, ready=nears[GRAD_AFTER], sent=g_sent, slack=15.0, done=g_there))
        k.add(hidden_back())
        k.add(work())
        k.add(plane_scatter(k, part, got, sx, sy, far=far, ready=parted, done=summed))
        k.add(norm_two())
        k.add(plane_gather(k, h2_own, h2_out, ready=h2_ready))

    ff_shape = (shape((2, line, 4, rows // 2, ff_q), BF16), ANY)
    plane = (shape((2, tokens, width), BF16), ANY)
    heads = (shape((2 * pairs // 2, length, 128), BF16), ANY)
    return call(
        body,
        [(x, VMEM), (gains, VMEM), (grad, ANY), (table, ANY), (bias, VMEM), (qkv, ANY), (out_w, ANY)]
        + [(gate, ANY), (up, ANY), (down, ANY)],
        [
            plane,
            plane,
            plane,
            (shape((tokens, width), F32), ANY),
            (shape((2, 3, line, 2, rows, cols_q), BF16), ANY),
            (shape((2, line, 2, rows, cols_q), BF16), ANY),
            ff_shape,
            ff_shape,
            ff_shape,
            heads,
            heads,
            heads,
            (shape((2, length, cols_q), BF16), ANY),
            (shape((2 * pairs // 2, 128, length), F32), ANY),
            (shape((2 * pairs // 2, 8, length), F32), VMEM),
            (shape((2, tokens, 128), F32), VMEM),
            (shape((2, 2, tokens, ff_q), BF16), ANY),
        ],
        [
            pltpu.VMEM((tokens, width), BF16),
            pltpu.VMEM((2, tokens, width), BF16),
            pltpu.VMEM((2,) + bias.shape, F32),
            pltpu.VMEM((2, 3, line, 2, rows, cols_q), BF16),
            pltpu.VMEM((2, line, 2, rows, cols_q), BF16),
            pltpu.VMEM((rows, ff), BF16),
            pltpu.VMEM((3, 4, 2, rows // 2, ff_q), BF16),
            pltpu.VMEM((length, 128), F32),
            pltpu.VMEM((length, 128), F32),
            pltpu.VMEM((length, 128), F32),
            pltpu.VMEM((2, length, 128), BF16),
            pltpu.VMEM((2, length, 128), BF16),
            pltpu.VMEM((2, length, 128), BF16),
            pltpu.VMEM((2, tokens, width), BF16),
        ]
        + scatter_scratch(tokens, width)
        + [pltpu.VMEM((tokens, width), F32), pltpu.VMEM((tokens, width), BF16)]
        + [pltpu.VMEM((2 * pairs // 2, length, 128), BF16) for _ in range(3)]
        + [
            pltpu.VMEM((2, length, cols_q), BF16),
            pltpu.VMEM((2 * pairs // 2, 128, length), F32),
            pltpu.VMEM((tokens, width), BF16),
            pltpu.VMEM((line, 4, rows // 2, ff_q), BF16),
            pltpu.VMEM((2, tokens, ff_q), BF16),
        ],
        line,
        1,
        120 + 10 * line_sems(line),
        62,
        "forward_kernel",
    )


def feed_kernel(line, h2, grad_all, w_gate, w_up, w_down, d_hid, resid, grad, gain):
    _, tokens, width = h2.shape
    length = 2 * tokens
    rows, ff_q = w_gate.shape[3:]
    chunk = 512

    def body(k, ins, outs, scratch):
        h2_in, g_in, w_gate, w_up, w_down, d_hid_in, resid, grad, gain = ins
        mixed_out, dr_out, dr_full, vectors, low_own, low_sib, high_own, high_sib, up_own, up_sib, got_down = outs
        h2, g, w, hid, d_gate, d_up, part, got, sx, sy, r_own, drb_own = scratch[:12]
        buffers, d_hid, free_down = scratch[12:-2], scratch[-2], scratch[-1]
        far, parted, summed, dr_ready, down_there = (Event() for _ in range(5))
        loads = {}

        def load(name, source, target):
            copy = k.local(source, target)
            copy.start()
            loads[name] = copy

        def weight(slot):
            return w[slot].reshape(width, ff_q)

        def half_weight(slot, side):
            return w[slot, side * line // 2 : (side + 1) * line // 2].reshape(width // 2, ff_q)

        def work():
            load("h2", h2_in, h2)
            for side in range(2):
                load(("gate", side), w_gate.at[side], w.at[side])
                load(("up", side), w_up.at[side], w.at[2 + side])
                if side == 0:
                    load("d_hid", d_hid_in, d_hid)
            load("g", g_in, g)
            for side in range(2):
                load(("down", side), w_down.at[side], w.at[4 + side])
            yield k.now + 5.0
            for index, (half, event) in enumerate(((1 - k.y, far), (k.y, parted))):

                @pl.loop(0, tokens // ROWS)
                def _(i):
                    at = pl.ds(pl.multiple_of(i * ROWS, ROWS), ROWS)

                    def need(name):
                        if index == 0:
                            pl.when(i == 0)(loads[name].wait)

                    need("h2")
                    rows_h = h2[half, at, :]
                    for side in range(2):
                        need(("gate", side))
                        gate_act = mm(rows_h, weight(side))
                        need(("up", side))
                        up_act = mm(rows_h, weight(2 + side))
                        if side == 0:
                            need("d_hid")
                        d_hidden = d_hid[side, half, at, :].astype(F32)
                        sigmoid_g = 1.0 / (1.0 + jnp.exp(-gate_act))
                        silu = gate_act * sigmoid_g
                        hid[side, half, at, :] = (silu * up_act).astype(BF16)
                        d_gate[side, half, at, :] = (
                            d_hidden * up_act * sigmoid_g * (1.0 + gate_act * (1.0 - sigmoid_g))
                        ).astype(BF16)
                        d_up[side, half, at, :] = (d_hidden * silu).astype(BF16)
                    for cols in range(2):
                        value = sum(
                            mm_nt(d_gate[side, half, at, :], half_weight(side, cols))
                            + mm_nt(d_up[side, half, at, :], half_weight(2 + side, cols))
                            for side in range(2)
                        )
                        part[half, at, cols * width // 2 : (cols + 1) * width // 2] = value.astype(BF16)

                k.now += 14.0
                k.fire(event)
                yield k.now
            pl.semaphore_signal(free_down, inc=1, device_id=k.sib, device_id_type=MESH)
            pl.semaphore_wait(free_down, 1)
            for name in ("g", ("down", 0), ("down", 1)):
                loads[name].wait()
            for quart in range(4):
                outer(g, ((hid, 0, 0), (hid, 1, 1)), quart)
                k.now += 1.7
                yield k.now
            k.fire(down_there)
            for half in range(2):
                for i in range(tokens // 512):
                    at = pl.ds(i * 512, 512)
                    for cols in range(2):
                        value = sum(mm_nt(hid[side, half, at, :], half_weight(4 + side, cols)) for side in range(2))
                        g[half, at, cols * width // 2 : (cols + 1) * width // 2] = value.astype(BF16)
                    k.now += 3.0
                    yield k.now
            keep = k.local(g, mixed_out)
            keep.start()
            stores = []
            for quart in range(4):
                outer(h2, ((d_gate, 0, 3), (d_gate, 1, 4)), quart)
                k.now += 1.7
                yield k.now
            stores = []
            for slot, first, target in ((3, 0, low_own), (4, 0, low_sib), (3, 1, high_own), (4, 1, high_sib)):
                stores.append(k.local(w.at[slot, :, :, pl.ds(first * rows // 2, rows // 2)], target))
                stores[-1].start()
            up_stores = []
            for batch in range(2):
                for store in up_stores:
                    store.wait()
                up_stores = []

                @pl.loop(0, length // chunk)
                def _(i):
                    turned = turn_columns(h2, batch * (length // chunk) + i)
                    at = pl.ds(pl.multiple_of(lax.rem(i, tokens // chunk) * chunk, chunk), chunk)
                    for side in range(2):
                        value = mm(turned, d_up[side].reshape(length, ff_q))
                        hid[side, i // (tokens // chunk), at, :] = value.astype(BF16)

                for side, target in enumerate((up_own, up_sib)):
                    for piece in range(length // rows):
                        index = batch * (length // rows) + piece
                        low = piece * rows
                        source = hid.at[side, low // tokens, pl.ds(low % tokens, rows)]
                        up_stores.append(k.local(source, target.at[index // 4, index % 4]))
                        up_stores[-1].start()
                k.now += 3.5
                yield k.now
            yield k.now + 3.0
            for store in stores + up_stores + [keep]:
                store.wait()

        def turn_columns(left, i):
            columns = left[:, :, pl.ds(pl.multiple_of(i * chunk, chunk), chunk)].reshape(length, chunk)
            return columns.astype(F32).T.astype(BF16)

        def outer(left, items, quart):
            count = width // chunk // 4

            @pl.loop(quart * count, quart * count + count)
            def _(i):
                turned = turn_columns(left, i)
                for right, side, slot in items:
                    store_rows(w, (slot,), i, mm(turned, right[side].reshape(length, ff_q)).astype(BF16), rows)

        def back():
            count = tokens // 4
            loads = [k.local(resid.at[pl.ds(i * count, count)], r_own.at[i % 2]) for i in range(4)]
            stores = [k.local(r_own.at[i % 2], dr_out.at[pl.ds(i * count, count)]) for i in range(4)]
            fetch = k.local(grad, drb_own)
            for copy in (fetch, loads[0], loads[1]):
                pl.when(k.home)(copy.start)
            vectors[...] = jnp.zeros_like(vectors)
            yield summed

            @pl.when(k.home)
            def _():
                fetch.wait()
                for i in range(4):
                    loads[i].wait()

                    def step(at):
                        full = pl.ds(pl.multiple_of(i * count + at.start, 16), 16)
                        value = scatter_sum(k, part, sx, sy, full)
                        scaled, inv_std = norm_rows(r_own[i % 2, at, :])
                        d_resid = drb_own[full, :].astype(F32) + norm_back(value, scaled, inv_std, gain[...])
                        r_own[i % 2, at, :] = d_resid
                        drb_own[full, :] = d_resid.astype(BF16)
                        vectors[0:8, :] += fold(value * scaled)
                        vectors[8:16, :] += fold(value)

                    rows_loop(count, 16, step)
                    stores[i].start()
                    if i in (1, 2):
                        stores[i - 1].wait()
                        loads[i + 1].start()

            k.now += 7.0
            k.fire(dr_ready)
            yield k.now + 5.0
            for store in stores[2:]:
                pl.when(k.home)(store.wait)

        k.add(work())
        k.add(plane_scatter(k, part, got, sx, sy, far=far, ready=parted, done=summed))
        k.add(back())
        k.add(plane_gather(k, drb_own, dr_full, ready=dr_ready))
        lower, upper = (0, rows // 2), (rows // 2, rows // 2)
        going = [Event() for _ in range(2)]
        down = (w.at[0], w.at[1], w.at[2]) + tuple(buffers[:2]) + (got_down,)
        k.add(line_scatter(k, *down, rows=lower, ready=(down_there,), following=going[0]))
        k.add(line_scatter(k, *down, rows=upper, ready=(going[0],)))

    grads = (shape((line, 4, rows, ff_q), BF16), ANY)
    half_grads = (shape((line, 4, rows // 2, ff_q), BF16), ANY)
    return call(
        body,
        [(item, ANY) for item in (h2, grad_all, w_gate, w_up, w_down, d_hid, resid, grad)] + [(gain, VMEM)],
        [
            (shape((2, tokens, width), BF16), ANY),
            (shape((tokens, width), F32), ANY),
            (shape((2, tokens, width), BF16), ANY),
            (shape((16, width), F32), VMEM),
            half_grads,
            half_grads,
            half_grads,
            half_grads,
            grads,
            grads,
            (shape((4, rows, ff_q), BF16), ANY),
        ],
        [
            pltpu.VMEM((2, tokens, width), BF16),
            pltpu.VMEM((2, tokens, width), BF16),
            pltpu.VMEM((6, line, 4, rows, ff_q), BF16),
            pltpu.VMEM((2, 2, tokens, ff_q), BF16),
            pltpu.VMEM((2, 2, tokens, ff_q), BF16),
            pltpu.VMEM((2, 2, tokens, ff_q), BF16),
            pltpu.VMEM((2, tokens, width), BF16),
        ]
        + scatter_scratch(tokens, width)
        + [pltpu.VMEM((2, tokens // 4, width), F32), pltpu.VMEM((tokens, width), BF16)]
        + line_scratch(line, rows, ff_q)[1:]
        + [pltpu.VMEM((2, 2, tokens, ff_q), BF16), pltpu.SemaphoreType.REGULAR],
        line,
        2,
        80 + 16 * line + 3 * line_sems(line),
        63,
        "feed_kernel",
    )


def attend_back_kernel(line, dr, w_out, w_qkv, q, key, v, lse, o_t, tables, mixed, resid, gate, up):
    _, tokens, width = dr.shape
    length = 2 * tokens
    cols_q = w_out.shape[-1]
    rows, ff_q = up[0].shape[2:]

    def body(k, ins, outs, scratch):
        dr_in, w_out, w_qkv, q, key, v, lse, o_t, tables, mixed, resid, gate_own, gate_sib, up_own, up_sib = ins
        dlin, bias, part_h, block_out, got_gate, got_up = outs
        wq, do, dq_t, dk, dv, cosine, sine_a, sine_b, key_marks, query_marks, marked = scratch[:11]
        part, got, sx, sy, r_own, out_own, dr = scratch[11:18]
        gate_line, up_line = scratch[18:22], scratch[22:26]
        loaded, summed = Event(), Event()

        def work():
            fetch_dr = k.local(dr_in, dr)
            fetch_dr.start()
            load = k.local(w_qkv, wq)
            load.start()
            bias[...] = jnp.zeros_like(bias)
            expand_tables(tables, cosine, sine_a, sine_b)
            mark_documents(tables, key_marks, query_marks)
            fetch_dr.wait()
            for slot in range(2):
                for half in range(2):

                    def project(at):
                        value = mm(dr[half, at, :], w_out[slot].reshape(width, cols_q)).astype(BF16)
                        full = pl.ds(pl.multiple_of(half * tokens + at.start, 256), at.size)
                        for pp in range(cols_q // 128):
                            do[slot * 2 + pp, full, :] = value[:, pp * 128 : pp * 128 + 128]

                    rows_loop(tokens, 512, project)
                k.now += 2.0
                yield k.now
                for pp in range(cols_q // 128):
                    pair = slot * 2 + pp
                    mark_keys(key, pair, key_marks, marked)
                    yield from attention_backward(
                        k, q, v, marked, query_marks, o_t, lse, do, dq_t, dk, dv, key, pair
                    )

                    def close(at):
                        cos, sin_a, sin_b = cosine[at, :], sine_a[at, :], sine_b[at, :]
                        dq = (dq_t[:, at].T * 0.125).astype(BF16).astype(F32)
                        dkk = dk[at, :].astype(BF16).astype(F32)
                        for j, value in enumerate(
                            (turn_lanes(dq, cos, -sin_a, -sin_b), turn_lanes(dkk, cos, -sin_a, -sin_b), dv[at, :])
                        ):
                            value = value.astype(BF16)
                            low = j * cols_q + pp * 128
                            dlin[slot, at, low : low + 128] = value
                            bias[slot, 0:1, low : low + 128] += jnp.sum(value.astype(F32), axis=0, keepdims=True)

                    rows_loop(length, 256, close)
                    k.now += 2.0
                    yield k.now
            load.wait()
            for half in range(2):

                def back(at):
                    full = pl.ds(pl.multiple_of(half * tokens + at.start, 256), at.size)
                    value = sum(
                        mm_nt(dlin[slot, full, j * cols_q : (j + 1) * cols_q], wq[slot, j].reshape(width, cols_q))
                        for slot in range(2)
                        for j in range(3)
                    )
                    dr[half, at, :] = value.astype(BF16)

                rows_loop(tokens, 512, back)
                k.now += 3.5
                yield k.now
            store = k.local(dr, part_h)
            store.start()
            yield k.now + 2.0
            store.wait()

        def fetch():
            copy = k.local(mixed, part)
            copy.start()
            half = tokens // 2
            loads = [k.local(resid.at[pl.ds(i * half, half)], r_own) for i in range(2)]
            pl.when(k.home)(loads[0].start)
            yield k.now + 2.0
            copy.wait()
            k.fire(loaded)
            yield summed

            @pl.when(k.home)
            def _():
                for i in range(2):
                    loads[i].wait()

                    def step(at):
                        full = pl.ds(pl.multiple_of(i * half + at.start, 16), 16)
                        out_own[full, :] = (r_own[at, :] + scatter_sum(k, part, sx, sy, full)).astype(BF16)

                    rows_loop(half, 16, step)
                    if i == 0:
                        loads[1].start()

            k.now += 2.0
            share = k.remote(out_own, block_out, k.sib)
            keep = k.local(out_own, block_out)
            share.start(k.home)
            pl.when(k.home)(keep.start)
            yield k.now + 8.0
            share.wait(k.away)
            pl.when(k.home)(keep.wait)

        going = [Event() for _ in range(2)]
        own, sib, from_dn, from_up = gate_line
        k.add(line_scatter(k, own, gate_sib, sib, from_dn, from_up, got_gate, own_part=gate_own, following=going[0], slack=8.0))
        own, sib, from_dn, from_up = up_line
        up = (own, up_sib, sib, from_dn, from_up, got_up)
        lower, upper = (0, rows // 2), (rows // 2, rows // 2)
        k.add(line_scatter(k, *up, rows=lower, own_part=up_own, ready=(going[0],), following=going[1], slack=8.0))
        k.add(line_scatter(k, *up, rows=upper, own_part=up_own, ready=(going[1],), slack=8.0))
        k.add(fetch())
        k.add(plane_scatter(k, part, got, sx, sy, far=loaded, done=summed))
        k.add(work())

    plane = (2, tokens, width)
    return call(
        body,
        [(dr, ANY), (w_out, VMEM), (w_qkv, ANY), (q, VMEM), (key, VMEM), (v, VMEM), (lse, VMEM), (o_t, VMEM)]
        + [(item, VMEM if item is tables else ANY) for item in (tables, mixed, resid) + gate + up],
        [
            (shape((2, length, 3 * cols_q), BF16), VMEM),
            (shape((2, 8, 3 * cols_q), F32), VMEM),
            (shape(plane, BF16), ANY),
            (shape((tokens, width), BF16), ANY),
            (shape((4, rows // 2, ff_q), BF16), ANY),
            (shape((4, rows, ff_q), BF16), ANY),
        ],
        [
            pltpu.VMEM(w_qkv.shape, BF16),
            pltpu.VMEM((4, length, 128), BF16),
            pltpu.VMEM((128, length), F32),
            pltpu.VMEM((length, 128), F32),
            pltpu.VMEM((length, 128), F32),
            pltpu.VMEM((length, 128), F32),
            pltpu.VMEM((length, 128), F32),
            pltpu.VMEM((length, 128), F32),
            pltpu.VMEM((2, length, 128), BF16),
            pltpu.VMEM((2, length, 128), BF16),
            pltpu.VMEM((2, length, 128), BF16),
            pltpu.VMEM(plane, BF16),
        ]
        + scatter_scratch(tokens, width)
        + [pltpu.VMEM((tokens // 2, width), F32), pltpu.VMEM((tokens, width), BF16), pltpu.VMEM(plane, BF16)]
        + [pltpu.VMEM((line, 4, rows // 2, ff_q), BF16)]
        + line_scratch(line, rows // 2, ff_q)
        + [pltpu.VMEM((line, 4, rows, ff_q), BF16)]
        + line_scratch(line, rows, ff_q),
        line,
        3,
        40 + 3 * line_sems(line),
        63,
        "attend_back_kernel",
    )


def last_kernel(line, part_h, x, gain, dr, vec_two, bias, h_one, dlin, dr_all, o, gate):
    _, tokens, width = part_h.shape
    length = 2 * tokens
    cols_q = o.shape[2]
    rows, ff_q = width // line // 4, gate[0].shape[3]
    chunk = 512

    def body(k, ins, outs, scratch):
        part_in, x, gain, dr, vec_two, bias, h_in, dlin, dr_all_in, o, gate_own, gate_sib = ins
        grad_in, vectors, got_qkv, got_out, got_gate = outs
        part, got, sx, sy, dr_own, in_own, partial, got_v, got_z, h_one, dr_all = scratch[:11]
        qkv_own, qkv_send, qkv_sib = scratch[11:14]
        qkv_rest = scratch[14:16]
        out_own, out_send, out_sib = scratch[16:19]
        out_rest = scratch[19:21]
        gate_mine, *gate_rest = scratch[21:25]
        h_turned = scratch[25]
        loaded, arrived, ready, out_there = (Event() for _ in range(4))
        qkv_there = [Event() for _ in range(3)]
        going = [Event() for _ in range(3)]

        def fetch():
            copy = k.local(part_in, part)
            copy.start()
            yield k.now + 1.0
            copy.wait()
            k.fire(loaded)

        def work():
            copies = [k.local(h_in, h_one), k.local(dr_all_in, dr_all)]
            for copy in copies:
                copy.start()
            yield k.now + 3.0
            for copy in copies:
                copy.wait()
            def turn(left, i):
                columns = left[:, :, pl.ds(pl.multiple_of(i * chunk, chunk), chunk)].reshape(length, chunk)
                return columns.astype(F32).T.astype(BF16)

            for j in range(3):

                @pl.loop(0, width // chunk)
                def _(i):
                    at = pl.ds(pl.multiple_of(i * chunk, chunk), chunk)
                    if j == 0:
                        h_turned[at, :] = turn(h_one, i)
                    for side, target in enumerate((qkv_own, qkv_send)):
                        value = mm(h_turned[at, :], dlin[side, :, j * cols_q : (j + 1) * cols_q])
                        store_rows(target, (j,), i, value.astype(BF16), rows)

                k.now += 4.5 if j == 0 else 3.0
                k.fire(qkv_there[j])
                yield k.now

            @pl.loop(0, width // chunk)
            def _(i):
                turned = turn(dr_all, i)
                for side, target in enumerate((out_own, out_send)):
                    store_rows(target, (), i, mm(turned, o[side]).astype(BF16), rows)

            k.now += 4.0
            k.fire(out_there)
            yield k.now

        def back():
            load = k.local(dr, dr_own)
            pl.when(k.home)(load.start)
            partial[...] = jnp.zeros_like(partial)
            yield arrived
            pl.when(k.home)(load.wait)

            @pl.when(k.home)
            def _():
                def step(at):
                    value = scatter_sum(k, part, sx, sy, at)
                    scaled, inv_std = norm_rows(x[at, :].astype(F32))
                    d_in = dr_own[at, :] + norm_back(value, scaled, inv_std, gain[...])
                    in_own[at, :] = d_in.astype(BF16)
                    partial[0:8, :] += fold(value * scaled)
                    partial[8:16, :] += fold(value)

                rows_loop(tokens, 16, step)

            k.now += 5.0
            k.fire(ready)
            share = k.remote(in_own, grad_in, k.sib)
            keep = k.local(in_own, grad_in)
            share.start(k.home)
            pl.when(k.home)(keep.start)
            yield k.now + 8.0
            share.wait(k.away)
            pl.when(k.home)(keep.wait)

        def reduce_vectors():
            yield ready
            vectors[...] = jnp.zeros_like(vectors)
            for i, (source, low) in enumerate(((partial, 0), (partial, 8), (vec_two, 0), (vec_two, 8))):
                vectors[i : i + 1, :] = jnp.sum(source[low : low + 8, :], axis=0, keepdims=True)
            for slot in range(2):
                tp = k.c if slot == 0 else 1 - k.c
                at = pl.ds(pl.multiple_of((tp * 4 + k.q) * cols_q, cols_q), cols_q)
                for j in range(3):
                    vectors[4 + j : 5 + j, at] = bias[slot, 0:1, j * cols_q : (j + 1) * cols_q]
            slot = 0
            for to in (k.sib, k.nx, k.ny):
                copy = k.remote(vectors, got_v.at[slot], to)
                copy.start(late=False)
                yield k.now + 4.0
                copy.wait()
                copy.gone()
                vectors[...] += got_v[slot]
                slot += 1
            spread = []
            for d in range(1, k.line):
                spread.append(k.remote(vectors, got_z.at[d - 1], k.at_line(d)))
                spread[-1].start(late=False)
            yield k.now + 6.0
            for copy in spread:
                copy.wait()
                copy.gone()
            for d in range(1, k.line):
                vectors[...] += got_z[d - 1]

        k.add(fetch())
        k.add(work())
        k.add(plane_scatter(k, part, got, sx, sy, far=loaded, done=arrived))
        k.add(back())
        k.add(reduce_vectors())
        k.add(line_scatter(k, gate_mine, gate_sib, *gate_rest, got_gate, own_part=gate_own))
        for j in range(3):
            items = [ref.at[j] for ref in (qkv_own, qkv_send, qkv_sib, *qkv_rest, got_qkv)]
            before = (going[j - 1],) if j else ()
            k.add(line_scatter(k, *items, ready=(qkv_there[j],) + before, following=going[j]))
        k.add(line_scatter(k, out_own, out_send, out_sib, *out_rest, got_out, ready=(out_there, going[2])))

    plane = (2, tokens, width)
    full_qkv, full_out = (3, line, 4, rows, cols_q), (line, 4, rows, cols_q)
    return call(
        body,
        [(part_h, ANY), (x, VMEM), (gain, VMEM), (dr, ANY), (vec_two, VMEM), (bias, VMEM), (h_one, ANY), (dlin, VMEM), (dr_all, ANY)]
        + [(o, VMEM)]
        + [(item, ANY) for item in gate],
        [(shape((tokens, width), BF16), ANY), (shape((8, width), F32), VMEM)]
        + [(shape(dims, BF16), ANY) for dims in ((3, 4, rows, cols_q), (4, rows, cols_q))]
        + [(shape((4, rows // 2, ff_q), BF16), ANY)],
        [pltpu.VMEM(plane, BF16)]
        + scatter_scratch(tokens, width)
        + [
            pltpu.VMEM((tokens, width), F32),
            pltpu.VMEM((tokens, width), BF16),
            pltpu.VMEM((16, width), F32),
            pltpu.VMEM((3, 8, width), F32),
            pltpu.VMEM((max(line - 1, 1), 8, width), F32),
            pltpu.VMEM(plane, BF16),
            pltpu.VMEM(plane, BF16),
        ]
        + [pltpu.VMEM(full_qkv, BF16), pltpu.VMEM(full_qkv, BF16)]
        + [pltpu.VMEM((3,) + piece.shape, BF16) for piece in line_scratch(line, rows, cols_q)]
        + [pltpu.VMEM(full_out, BF16), pltpu.VMEM(full_out, BF16)]
        + line_scratch(line, rows, cols_q)
        + [pltpu.VMEM((line, 4, rows // 2, ff_q), BF16)]
        + line_scratch(line, rows // 2, ff_q)
        + [pltpu.VMEM((width, length), BF16)],
        line,
        4,
        60 + 6 * line_sems(line),
        63,
        "last_kernel",
    )


def unquarter(got):
    return jnp.concatenate([got[i] for i in range(4)], axis=1).astype(F32)


def shards(
    fsdp_size,
    block_in,
    segments,
    positions,
    gain_one,
    shift_one,
    qkv_weight,
    qkv_bias,
    out_weight,
    gain_two,
    shift_two,
    gate_weight,
    up_weight,
    down_weight,
    grad_out,
):
    line = fsdp_size // 2
    seq_local, tokens, width = block_in.shape
    head_size = qkv_bias.shape[2]
    heads_tp = qkv_bias.shape[1]
    cols_tp = heads_tp * head_size
    cols_q = cols_tp // 4
    length = 2 * tokens

    fsdp = lax.axis_index("fsdp")
    ctx = lax.axis_index("ctx")
    core = lax.axis_index("tp")
    place = fsdp % 2
    quarter = place * 2 + ctx

    x = block_in.reshape(tokens, width)
    grad = grad_out.reshape(tokens, width)
    row = lax.broadcasted_iota(jnp.int32, (8, width), 0)
    gains = jnp.zeros((8, width), F32)
    for i, vector in enumerate((gain_one, shift_one, gain_two, shift_two)):
        gains = jnp.where(row == i, vector.astype(F32)[None], gains)
    lane = jnp.arange(128, dtype=jnp.int32)
    spot = lane % head_size
    half = ROT // 2
    frequency = THETA ** (-(2.0 * (spot % half).astype(F32)) / ROT)
    angle = positions.reshape(tokens, 1).astype(F32) * frequency[None]
    turned = (spot < ROT)[None]
    table = jnp.where(
        (lane < head_size)[None], jnp.where(turned, jnp.cos(angle), 1.0), jnp.where(turned, jnp.sin(angle), 0.0)
    )
    table = jnp.where((lane == 32)[None], segments.reshape(tokens, 1).astype(F32), table)
    bias = lax.dynamic_slice_in_dim(qkv_bias.reshape(3, cols_tp), quarter * cols_q, cols_q, axis=1).astype(F32)
    bias = jnp.concatenate([bias, jnp.zeros((5, cols_q), F32)], axis=0)
    qkv = qkv_weight.transpose(1, 0, 2)

    (h_one, grad_all, h_two, resid, w_qkv, w_out, w_gate, w_up, w_down, q, key, v, attn, attn_t, lse, tables, d_hid) = forward_kernel(
        line, x, gains, grad, table, bias, qkv, out_weight, gate_weight, up_weight, down_weight
    )
    mixed, d_resid, dr_all, vec_two, low_own, low_sib, high_own, high_sib, up_own, up_sib, got_down = feed_kernel(
        line, h_two, grad_all, w_gate, w_up, w_down, d_hid, resid, grad, gains[2:3]
    )
    dlin, d_bias, d_h_one, block_out, got_gate_upper, got_up = attend_back_kernel(
        line,
        dr_all,
        w_out,
        w_qkv,
        q,
        key,
        v,
        lse,
        attn_t,
        tables,
        mixed,
        resid,
        (high_own, high_sib),
        (up_own, up_sib),
    )

    d_in, vectors, got_qkv, got_out, got_gate_lower = last_kernel(
        line, d_h_one, x, gains[0:1], d_resid, vec_two, d_bias, h_one, dlin, dr_all, attn, (low_own, low_sib)
    )
    got_gate = jnp.concatenate([got_gate_lower, got_gate_upper], axis=1)

    share = fsdp * 2 + ctx
    share_size = width // (2 * fsdp_size)
    shares = lax.dynamic_slice_in_dim(vectors[:4], share * share_size, share_size, axis=1)
    bias_size = head_size // (2 * fsdp_size)
    d_bias = vectors[4:7].reshape(3, 2, heads_tp, head_size)
    d_bias = lax.dynamic_slice(d_bias, (0, core, 0, share * bias_size), (3, 1, heads_tp, bias_size))
    d_qkv = jnp.concatenate([got_qkv[:, i] for i in range(4)], axis=2).astype(F32).transpose(1, 0, 2)
    return (
        block_out.reshape(seq_local, tokens, width),
        d_in.astype(F32).reshape(seq_local, tokens, width),
        shares[0],
        shares[1],
        d_qkv,
        d_bias.reshape(3, heads_tp, bias_size),
        unquarter(got_out),
        shares[2],
        shares[3],
        unquarter(got_gate),
        unquarter(got_up),
        unquarter(got_down),
    )


def solution(mesh):
    placed = (
        P("fsdp", "ctx", None),
        P("fsdp", "ctx"),
        P("fsdp", "ctx"),
        P(),
        P(),
        P("fsdp", None, "tp"),
        P(None, "tp", None),
        P("fsdp", "tp"),
        P(),
        P(),
        P("fsdp", "tp"),
        P("fsdp", "tp"),
        P("fsdp", "tp"),
        P("fsdp", "ctx", None),
    )

    def run(*arrays):
        return shards(mesh.shape["fsdp"], *arrays)

    return jax.shard_map(
        run,
        mesh=mesh,
        in_specs=placed,
        out_specs=(
            P("fsdp", "ctx", None),
            P("fsdp", "ctx", None),
            P(("fsdp", "ctx")),
            P(("fsdp", "ctx")),
            P(("fsdp", "ctx"), None, "tp"),
            P(None, "tp", ("fsdp", "ctx")),
            P(("fsdp", "ctx"), "tp"),
            P(("fsdp", "ctx")),
            P(("fsdp", "ctx")),
            P(("fsdp", "ctx"), "tp"),
            P(("fsdp", "ctx"), "tp"),
            P(("fsdp", "ctx"), "tp"),
        ),
        check_vma=False,
    )
```

time: 3370 us -> 628 us (0.19)
  waiting for transfers between devices: 2670 us -> 0 us
  Pallas kernels: 0 us -> 589 us
  matrix products: 263 us -> 0 us
  blocking collectives: 140 us -> 0 us
  local copies, waits for them, and re-layouts: 137 us -> 12.2 us
  other arithmetic: 108 us -> 15 us
    reduce_scatter x5 -> x0, waiting for transfers between devices: 1980 us -> none  [the longest x1 518 us: shards(): lax.psum_scatter(d_qkv_w, ('fsdp', 'ctx'), scatter_dimension=0, tiled=True)]
    all_gather x5 -> x0, waiting for transfers between devices: 644 us -> none  [the longest x1 178 us: shards(): lax.all_gather(qkv_weight, 'fsdp', axis=0, tiled=True)]
    pallas_call x0 -> x4, Pallas kernels: none -> 589 us  [call(): pl.pallas_call(run, out_shape=[out for out, _ in outs], in_specs=[spec fo...]
    dot_general x71 -> x0, matrix products: 263 us -> none  [the longest x16 32.8 us: unit_scores(): jnp.einsum('qd,kd->qk', queries, key_rows, preferred_element_type=jnp.flo...]
    unnamed x1 -> x0, blocking collectives: 93.4 us -> none
    unnamed x9 -> x0, other arithmetic: 65.2 us -> none
    unnamed x121 -> x16, local copies, waits for them, and re-layouts: 63.2 us -> 1.38 us
    psum x3 -> x0, waiting for transfers between devices: 44.6 us -> none  [the longest x1 25 us: shards(): branch = lax.psum(branch_part, 'tp')]
  transfers between devices with their start and end apart: 19 -> 0, of which waited for: 11 -> 0; matrix products, arithmetic and copies ran while one was open for 8% -> 0% of each run, Pallas kernels for 0% -> 0%
where the time goes in v1:
time: 628 us; the launch traced here: 617 us
  Pallas kernels  589 us (94%)
  other arithmetic  15 us (2%)
  local copies, waits for them, and re-layouts  12.2 us (2%)
    pallas_call x4, Pallas kernels, call(): pl.pallas_call(run, out_shape=[out for out, _ in outs], in_specs=[spec fo...  589 us

profile of v1, /device:TPU:0, one launch (start us, length us, event | category | flops | bytes accessed | tf_op | source)
XLA Modules:
  0.0 617.1 jit_solution(16605420667423965614)
XLA Ops:
  2.1 0.7 convert_element_type.59
  2.8 0.7 convert_element_type.58
  3.5 0.8 reshape.108
  4.9 0.7 convert_element_type.57
  5.6 0.7 convert_element_type.56
  7.0 1.9 fusion.2.refs_3_
  8.9 247.0 %forward_kernel.1 = (bf16[2,512,2048]{2,1,0:T(8,128)(2,1)}, bf16[2,512,2048]{2,1,0:T(8,128)(2,1)}, bf16[2,512,2048]{2,1,0:T(8,128)(2,1)}, f32[512,2048]{1,0:T(8,...) custom-call(bf16[512,2048]{1,0:T(8,128)(2,1)} %bitcast.62, ...), custom_call_target="tpu_custom_call" | custom-call | tf_op jit(solution)/shard_map/forward_kernel/pallas_call | solution.py:220
  255.8 126.3 %feed_kernel.1 = (bf16[2,512,2048]{2,1,0:T(8,128)(2,1)}, f32[512,2048]{1,0:T(8,128)}, bf16[2,512,2048]{2,1,0:T(8,128)(2,1)}, f32[16,2048]{1,0:T(8,128)}, bf16[4,...) custom-call(bf16[2,512,2048]{2,1,0:T(8,128)(2,1)} %get-tuple-element, ...), custom_call_target="tpu_custom_call" | custom-call | tf_op jit(solution)/shard_map/feed_kernel/pallas_call | solution.py:220
  382.2 96.4 %attend_back_kernel.1 = (bf16[2,1024,768]{2,1,0:T(8,128)(2,1)}, f32[2,8,768]{2,1,0:T(8,128)}, bf16[2,512,2048]{2,1,0:T(8,128)(2,1)}, bf16[512,2048]{1,0:T(8,128)...) custom-call(bf16[2,512,2048]{2,1,0:T(8,128)(2,1)} %get-tuple-element.58.refs_0_.refs_8_, ...), custom_call_target="tpu_custom_call" | custom-call | tf_op jit(solution)/shard_map/attend_back_kernel/pallas_call | solution.py:220
  478.6 119.1 %last_kernel.1 = (bf16[512,2048]{1,0:T(8,128)(2,1)}, f32[8,2048]{1,0:T(8,128)}, bf16[3,4,128,256]{3,2,1,0:T(8,128)(2,1)}, bf16[4,128,256]{2,1,0:T(8,128)(2,1)}, bf16[4,64,704]{2,1,0:T(8,128)(2,1)}) custom-call(bf16[2,512,2048]{2,1,0:T(8,128)(2,1)} %get-tuple-element.73.refs_0_, bf16[512,2048]{1,0:T(8,128)(2,1)} %bitcast.63, ...), custom_call_target="tpu_custom_call" | custom-call | tf_op jit(solution)/shard_map/last_kernel/pallas_call | solution.py:220
  597.7 0.8 slice.93
  598.6 0.8 slice.86
  600.8 0.9 slice_bitcast_fusion.15
  601.7 1.2 slice_bitcast_fusion.6
  602.9 1.0 slice_bitcast_fusion.19
  603.9 0.8 maximum_convert_fusion
  604.8 1.3 convert_bitcast_fusion
  606.7 1.2 convert_element_type.66
  608.5 1.2 convert_element_type.67
  609.7 0.7 slice_bitcast_fusion.7
  610.4 1.4 concatenate.30
  611.8 1.2 convert_element_type.68
  613.0 2.5 bitcast_convert_fusion
  615.6 1.3 copy.34
  (36 shorter events, 5.2 us)
Async XLA Ops:
  6.3 2.5 copy-start.6
  602.9 3.2 copy-start.5
  603.9 2.2 copy-start.4
  606.3 1.7 copy-start.3
  608.0 1.7 copy-start.2
  610.4 2.6 copy-start
  613.0 2.5 copy-start.1
